TPU v7x, 512 devices: a whole 4x8x8 slice. The times are simulated.
512 devices in a mesh: depth: 64 (over y, x, core), tile: 8 (over z).
Axes of the slice: x: 4, y: 8, z: 8, core: 2. Of those that a mesh axis runs over, the one named last changes fastest.
Arguments:
- volume: bfloat16 [1024, 512, 1024], P('depth', 'tile'), may hold values from 0 to 1
- empty_slices: int32 [64, 8], P('depth'), may hold values from 0 to 16
- shear: int32 [2], replicated, may hold values from 1 to 7
- extinction: float32 [1], replicated, may hold values from 0.25 to 1
- palette: float32 [2, 3], replicated, may hold values from 0.2 to 1.5
Outputs:
- image: float32 [4, 512, 1024], P(None, 'tile')
All inputs are finite; a program needn't handle non-finite values.
Results may differ from a plain program's by a relative error of at most 0.0003.
Values may be sent and summed in bfloat16 or wider, within the bound.
No kernel may reach another device: no remote copies, remote signals or barrier semaphores. Data moves between devices by JAX's collectives and lax.ppermute only.
A program may use at most 64 MiB of HBM per device.

v0:
```python
import jax
import jax.numpy as jnp
from jax import lax
from jax.sharding import PartitionSpec as P


def shifted(block, axis, distance):
    devices = range(lax.axis_size(axis))
    route = [(i - distance, i) for i in devices if i - distance in devices]
    return lax.ppermute(block, axis, route)


def partner(value, axis, apart):
    mask = 2**apart
    pairs = [(source, source ^ mask) for source in range(lax.axis_size(axis))]
    return lax.ppermute(value, axis, pairs)


def resample(padded, shear, depth_pos, depth_total, row_span, width, out_rows):
    col_num = shear[0] * depth_pos * width
    col_den = 32 * depth_total
    col_shift = col_num // col_den
    col_frac = (col_num % col_den).astype(jnp.float32) / float(col_den)
    row_num = shear[1] * depth_pos * row_span
    row_den = 8 * depth_total
    row_shift = row_num // row_den
    row_frac = (row_num % row_den).astype(jnp.float32) / float(row_den)
    col_pad = width // 4

    def pick_at(row_step, col_step):
        start_row = row_span - row_shift - row_step
        start_col = col_pad - col_shift - col_step
        return lax.dynamic_slice(padded, (start_row, start_col), (out_rows, width))

    upper_line = (1.0 - col_frac) * pick_at(0, 0) + col_frac * pick_at(0, 1)
    lower_line = (1.0 - col_frac) * pick_at(1, 0) + col_frac * pick_at(1, 1)
    return (1.0 - row_frac) * upper_line + row_frac * lower_line


def classify(sample, extinction, palette, depth_total):
    sigma = extinction[0] * 4.0 / depth_total
    alpha = 1.0 - jnp.exp(-sigma * sample)
    emitted = alpha[None] * (palette[0][:, None, None] + palette[1][:, None, None] * sample[None])
    return (alpha, emitted)


def composite(front, back):
    color = front[:3] + front[3:4] * back[:3]
    trans = front[3:4] * back[3:4]
    return jnp.concatenate([color, trans], axis=0)


def unscramble(whole, bit_count, piece_len):
    shaped = whole.reshape((4,) + (2,) * bit_count + (piece_len,))
    order = (0,) + tuple(range(bit_count, 0, -1)) + (bit_count + 1,)
    return jnp.transpose(shaped, order).reshape(4, -1)


def per_device(volume, empty_slices, shear, extinction, palette):
    slab, rows, width = volume.shape
    depth_count = lax.axis_size("depth")
    depth_total = slab * depth_count
    below = shifted(volume, "tile", 1)
    tile_pos = lax.axis_index("tile")
    depth_idx = lax.axis_index("depth")
    count_row = empty_slices[0]
    own_count = lax.dynamic_index_in_dim(count_row, tile_pos, 0, keepdims=False)
    prior_count = lax.dynamic_index_in_dim(
        count_row, jnp.maximum(tile_pos - 1, 0), 0, keepdims=False
    )
    lower_count = jnp.where(tile_pos > 0, prior_count, slab)
    first_live = jnp.minimum(own_count, lower_count)

    def advance(slice_idx, carry):
        color, trans = carry
        depth_pos = depth_idx * slab + slice_idx
        own_plane = lax.dynamic_index_in_dim(volume, slice_idx, 0, keepdims=False).astype(
            jnp.float32
        )
        low_plane = lax.dynamic_index_in_dim(below, slice_idx, 0, keepdims=False).astype(
            jnp.float32
        )
        own_plane = jnp.where(slice_idx >= own_count, own_plane, jnp.float32(0.0))
        low_plane = jnp.where(slice_idx >= lower_count, low_plane, jnp.float32(0.0))
        padded = jnp.pad(jnp.concatenate([low_plane, own_plane], axis=0), ((0, 0), (width // 4, 0)))
        sample = resample(padded, shear, depth_pos, depth_total, rows, width, rows)
        alpha, emitted = classify(sample, extinction, palette, depth_total)
        color = color + trans[None] * emitted
        trans = trans * (1.0 - alpha)
        return (color, trans)

    start = (jnp.zeros((3, rows, width), jnp.float32), jnp.ones((rows, width), jnp.float32))
    color, trans = lax.fori_loop(first_live, slab, advance, start)
    partial_image = jnp.concatenate([color, trans[None]], axis=0).reshape(4, rows * width)
    bit_count = depth_count.bit_length() - 1
    piece_len = rows * width // depth_count
    current = partial_image
    for bit_index in range(bit_count):
        upper = depth_idx >> bit_index & 1 == 1
        half = current.shape[1] // 2
        first_half = current[:, :half]
        second_half = current[:, half:]
        keep = jnp.where(upper, second_half, first_half)
        outgoing = jnp.where(upper, first_half, second_half)
        received = partner(outgoing, "depth", bit_index)
        front = jnp.where(upper, received, keep)
        back = jnp.where(upper, keep, received)
        current = composite(front, back)
    whole = lax.all_gather(current, "depth", axis=1, tiled=True)
    whole = unscramble(whole, bit_count, piece_len)
    whole = whole.reshape(4, rows, width)
    return jnp.concatenate([whole[:3], 1.0 - whole[3:4]], axis=0)


def solution(mesh):
    in_specs = (P("depth", "tile", None), P("depth", None), P(), P(), P())
    out_specs = P(None, "tile", None)
    return jax.shard_map(
        per_device, mesh=mesh, in_specs=in_specs, out_specs=out_specs, check_vma=False
    )
```

profile of v0, /device:TPU:1, one launch (start us, length us, event | category | flops | bytes accessed | tf_op | source)
XLA Modules:
  0.0 286.9 jit_solution(2535379172469783899)
XLA Ops:
  6.5 4.9 %collective-permute-start = (bf16[16,64,1024]{2,1,0:T(8,128)(2,1)}, bf16[16,64,1024]{2,1,0:T(8,128)(2,1)S(1)}, u32[]{:S(2)}, u32[]{:S(2)}) collective-permute-start(bf16[16,64,1024]{2,1,0:T(8,128)(2,1)} %param.7), channel_id=1, source_target_pairs={{0,1},{1,2},{2,3},{3,4},{4,5},{5,6},{6,7},{8,9},{9,10},{10,11},{11... | collective-permute-start | bytes 6291464 | tf_op jit(solution)/shard_map/ppermute | solution.py:10
  12.2 1.4 constant_dynamic-slice_fusion
  14.8 38.8 %collective-permute-done = bf16[16,64,1024]{2,1,0:T(8,128)(2,1)S(1)} collective-permute-done((bf16[16,64,1024]{2,1,0:T(8,128)(2,1)}, bf16[16,64,1024]{2,1,0:T(8,128)(2,1)S(1)}, u32[]{:S(2)}, u32[]{:S(2)}) %collective-permute-start) | collective-permute-done | bytes 2097184 | tf_op jit(solution)/shard_map/ppermute | solution.py:10
  53.6 25.8 %while.17 = (s32[]{:T(128)}, f32[3,64,1024]{2,1,0:T(8,128)S(1)}, f32[64,1024]{1,0:T(8,128)S(1)}, f32[]{:T(128)}, s32[2]{0:T(128)}, /*index=5*/s32[]{:T(128)}, s3...) while((s32[]{:T(128)}, f32[3,64,1024]{2,1,0:T(8,128)S(1)}, ...), condition=%wide.region_1.2_spmd, body=%wide.region_0.1_spmd.sunk | while | flops 2752584 | bytes 6948089 | solution.py:93
  53.7 1.3 fusion.20
  56.9 1.0 select_bitcast_fusion.3
  57.9 0.4 subtract_multiply_fusion.2
  58.3 0.4 multiply_add_fusion.4
  58.8 1.3 fusion.20
  62.1 1.0 select_bitcast_fusion.3
  63.1 0.4 subtract_multiply_fusion.2
  63.5 0.4 multiply_add_fusion.4
  64.0 1.3 fusion.20
  67.2 1.0 select_bitcast_fusion.3
  68.2 0.4 subtract_multiply_fusion.2
  68.6 0.4 multiply_add_fusion.4
  69.1 1.3 fusion.20
  72.4 1.0 select_bitcast_fusion.3
  73.4 0.4 subtract_multiply_fusion.2
  73.8 0.4 multiply_add_fusion.4
  74.3 1.3 fusion.20
  77.5 1.0 select_bitcast_fusion.3
  78.5 0.4 subtract_multiply_fusion.2
  78.9 0.4 multiply_add_fusion.4
  79.4 0.5 copy.9
  79.9 0.3 copy.10
  80.2 0.5 broadcast_select_fusion.3
  80.7 57.5 %collective-permute-start.1 = (f32[4,32768]{1,0:T(4,128)S(1)}, f32[4,32768]{1,0:T(4,128)S(1)}, u32[]{:S(2)}, u32[]{:S(2)}) collective-permute-start(f32[4,32768]{1,0:T(4,128)S(1)} %get-tuple-element.332), channel_id=1, source_target_pairs={{0,8},{8,0},{16,24},{24,16},{32,40},{40,32},{48,56},{56,48},{64,72... | collective-permute-start | bytes 1572872 | tf_op jit(solution)/shard_map/ppermute | solution.py:16
  138.2 1.5 collective-permute-done.1
  139.7 0.4 broadcast_select_fusion.1
  140.1 0.3 fusion.13
  140.8 3.0 %collective-permute-start.2 = (f32[4,16384]{1,0:T(4,128)S(1)}, f32[4,16384]{1,0:T(4,128)S(1)}, u32[]{:S(2)}, u32[]{:S(2)}) collective-permute-start(f32[4,16384]{1,0:T(4,128)S(1)} %get-tuple-element.330), channel_id=1, source_target_pairs={{0,16},{8,24},{16,0},{24,8},{32,48},{40,56},{48,32},{56,40},{64,80... | collective-permute-start | bytes 786440 | tf_op jit(solution)/shard_map/ppermute | solution.py:16
  143.9 6.4 %collective-permute-done.2 = f32[4,16384]{1,0:T(4,128)S(1)} collective-permute-done((f32[4,16384]{1,0:T(4,128)S(1)}, f32[4,16384]{1,0:T(4,128)S(1)}, u32[]{:S(2)}, u32[]{:S(2)}) %collective-permute-start.2) | collective-permute-done | bytes 262176 | tf_op jit(solution)/shard_map/ppermute | solution.py:16
  150.8 3.6 %collective-permute-start.3 = (f32[4,8192]{1,0:T(4,128)S(1)}, f32[4,8192]{1,0:T(4,128)S(1)}, u32[]{:S(2)}, u32[]{:S(2)}) collective-permute-start(f32[4,8192]{1,0:T(4,128)S(1)} %get-tuple-element.328), channel_id=1, source_target_pairs={{0,32},{8,40},{16,48},{24,56},{32,0},{40,8},{48,16},{56,24},{64,96... | collective-permute-start | bytes 393224 | tf_op jit(solution)/shard_map/ppermute | solution.py:16
  154.5 3.6 %collective-permute-done.3 = f32[4,8192]{1,0:T(4,128)S(1)} collective-permute-done((f32[4,8192]{1,0:T(4,128)S(1)}, f32[4,8192]{1,0:T(4,128)S(1)}, u32[]{:S(2)}, u32[]{:S(2)}) %collective-permute-start.3) | collective-permute-done | bytes 131104 | tf_op jit(solution)/shard_map/ppermute | solution.py:16
  158.4 8.3 %collective-permute-start.4 = (f32[4,4096]{1,0:T(4,128)S(1)}, f32[4,4096]{1,0:T(4,128)S(1)}, u32[]{:S(2)}, u32[]{:S(2)}) collective-permute-start(f32[4,4096]{1,0:T(4,128)S(1)} %get-tuple-element.326), channel_id=1, source_target_pairs={{0,64},{8,72},{16,80},{24,88},{32,96},{40,104},{48,112},{56,120},{... | collective-permute-start | bytes 196616 | tf_op jit(solution)/shard_map/ppermute | solution.py:16
  166.6 1.6 collective-permute-done.4
  168.4 4.7 %collective-permute-start.5 = (f32[4,2048]{1,0:T(4,128)S(1)}, f32[4,2048]{1,0:T(4,128)S(1)}, u32[]{:S(2)}, u32[]{:S(2)}) collective-permute-start(f32[4,2048]{1,0:T(4,128)S(1)} %get-tuple-element.324), channel_id=1, source_target_pairs={{0,128},{8,136},{16,144},{24,152},{32,160},{40,168},{48,176},{56,1... | collective-permute-start | bytes 98312 | tf_op jit(solution)/shard_map/ppermute | solution.py:16
  173.1 1.3 collective-permute-done.5
  174.5 5.9 %collective-permute-start.6 = (f32[4,1024]{1,0:T(4,128)S(1)}, f32[4,1024]{1,0:T(4,128)S(1)}, u32[]{:S(2)}, u32[]{:S(2)}) collective-permute-start(f32[4,1024]{1,0:T(4,128)S(1)} %get-tuple-element.322), channel_id=1, source_target_pairs={{0,256},{8,264},{16,272},{24,280},{32,288},{40,296},{48,304},{56,3... | collective-permute-start | bytes 49160 | tf_op jit(solution)/shard_map/ppermute | solution.py:16
  180.4 2.5 collective-permute-done.6
  183.0 0.6 pad_maximum_fusion.7
  183.6 91.3 %all-gather.2.cloned.1.call-done = f32[4,65536]{1,0:T(4,128)} async-done(((f32[4,1024]{1,0:T(4,128)}), f32[4,65536]{1,0:T(4,128)}) %all-gather.2.cloned.1.call-update) | async-done | bytes 1048592 | tf_op jit(solution)/shard_map/all_gather | solution.py:109
  274.9 2.3 reshape.43
  277.5 0.6 copy.6
  278.1 0.5 slice.201
  278.6 0.3 copy.7
  279.0 1.0 pad_maximum_fusion
  (53 shorter events, 2.3 us)
Async XLA Ops:
  6.5 268.4 %all-gather.2.cloned.1.call-start = ((), (), s32[]{:S(2)}) async-start(), calls=%async_computation | async-start | bytes 1064960 | tf_op jit(solution)/shard_map/all_gather | solution.py:109
  6.5 47.0 %collective-permute-start = (bf16[16,64,1024]{2,1,0:T(8,128)(2,1)}, bf16[16,64,1024]{2,1,0:T(8,128)(2,1)S(1)}, u32[]{:S(2)}, u32[]{:S(2)}) collective-permute-start(bf16[16,64,1024]{2,1,0:T(8,128)(2,1)} %param.7), channel_id=1, source_target_pairs={{0,1},{1,2},{2,3},{3,4},{4,5},{5,6},{6,7},{8,9},{9,10},{10,11},{11... | collective-permute-start | bytes 6291464 | tf_op jit(solution)/shard_map/ppermute | solution.py:10
  55.6 2.8 copy-start
  60.7 2.8 copy-start
  65.9 2.8 copy-start
  71.0 2.8 copy-start
  76.2 2.8 copy-start
  80.7 59.0 %collective-permute-start.1 = (f32[4,32768]{1,0:T(4,128)S(1)}, f32[4,32768]{1,0:T(4,128)S(1)}, u32[]{:S(2)}, u32[]{:S(2)}) collective-permute-start(f32[4,32768]{1,0:T(4,128)S(1)} %get-tuple-element.332), channel_id=1, source_target_pairs={{0,8},{8,0},{16,24},{24,16},{32,40},{40,32},{48,56},{56,48},{64,72... | collective-permute-start | bytes 1572872 | tf_op jit(solution)/shard_map/ppermute | solution.py:16
  140.8 9.4 %collective-permute-start.2 = (f32[4,16384]{1,0:T(4,128)S(1)}, f32[4,16384]{1,0:T(4,128)S(1)}, u32[]{:S(2)}, u32[]{:S(2)}) collective-permute-start(f32[4,16384]{1,0:T(4,128)S(1)} %get-tuple-element.330), channel_id=1, source_target_pairs={{0,16},{8,24},{16,0},{24,8},{32,48},{40,56},{48,32},{56,40},{64,80... | collective-permute-start | bytes 786440 | tf_op jit(solution)/shard_map/ppermute | solution.py:16
  150.8 7.2 %collective-permute-start.3 = (f32[4,8192]{1,0:T(4,128)S(1)}, f32[4,8192]{1,0:T(4,128)S(1)}, u32[]{:S(2)}, u32[]{:S(2)}) collective-permute-start(f32[4,8192]{1,0:T(4,128)S(1)} %get-tuple-element.328), channel_id=1, source_target_pairs={{0,32},{8,40},{16,48},{24,56},{32,0},{40,8},{48,16},{56,24},{64,96... | collective-permute-start | bytes 393224 | tf_op jit(solution)/shard_map/ppermute | solution.py:16
  158.4 9.9 %collective-permute-start.4 = (f32[4,4096]{1,0:T(4,128)S(1)}, f32[4,4096]{1,0:T(4,128)S(1)}, u32[]{:S(2)}, u32[]{:S(2)}) collective-permute-start(f32[4,4096]{1,0:T(4,128)S(1)} %get-tuple-element.326), channel_id=1, source_target_pairs={{0,64},{8,72},{16,80},{24,88},{32,96},{40,104},{48,112},{56,120},{... | collective-permute-start | bytes 196616 | tf_op jit(solution)/shard_map/ppermute | solution.py:16
  168.4 6.0 %collective-permute-start.5 = (f32[4,2048]{1,0:T(4,128)S(1)}, f32[4,2048]{1,0:T(4,128)S(1)}, u32[]{:S(2)}, u32[]{:S(2)}) collective-permute-start(f32[4,2048]{1,0:T(4,128)S(1)} %get-tuple-element.324), channel_id=1, source_target_pairs={{0,128},{8,136},{16,144},{24,152},{32,160},{40,168},{48,176},{56,1... | collective-permute-start | bytes 98312 | tf_op jit(solution)/shard_map/ppermute | solution.py:16
  174.5 8.4 %collective-permute-start.6 = (f32[4,1024]{1,0:T(4,128)S(1)}, f32[4,1024]{1,0:T(4,128)S(1)}, u32[]{:S(2)}, u32[]{:S(2)}) collective-permute-start(f32[4,1024]{1,0:T(4,128)S(1)} %get-tuple-element.322), channel_id=1, source_target_pairs={{0,256},{8,264},{16,272},{24,280},{32,288},{40,296},{48,304},{56,3... | collective-permute-start | bytes 49160 | tf_op jit(solution)/shard_map/ppermute | solution.py:16
Sparse Core Ops, SparseCore 0:
  183.7 91.1 all-gather.1
where the time goes:
time: 288 us; the launch traced here: 287 us
  waiting for transfers between devices  147 us (51%)
  starting transfers between devices  87.9 us (31%)
  between operations  15.6 us (5%)
  other arithmetic  13.4 us (5%)
  local copies, waits for them, and re-layouts  12.8 us (4%)
  loops' own time  10.2 us (4%)
    all_gather x1, waiting for transfers between devices, per_device(): whole = lax.all_gather(current, 'depth', axis=1, tiled=True)  91.3 us
    ppermute x6, starting transfers between devices, partner(): return lax.ppermute(value, axis, pairs)  83 us
    ppermute x1, waiting for transfers between devices, shifted(): return lax.ppermute(block, axis, route)  38.8 us
    ppermute x6, waiting for transfers between devices, partner(): return lax.ppermute(value, axis, pairs)  16.9 us
    another operation x1, loops' own time, per_device(): color, trans = lax.fori_loop(first_live, slab, advance, start)  10.2 us
    slice x5, local copies, waits for them, and re-layouts, resample(): col_num = shear[0] * depth_pos * width  6.56 us
  transfers between devices with their start and end apart: 8, of which 8 were waited for; matrix products, arithmetic and copies ran while one was open for 0% of the time, Pallas kernels for 0%

commit v1 on v0

v1 whole, which is shorter than its diff:
```python
import functools
import math

import jax
import jax.numpy as jnp
from jax import lax
from jax.experimental import pallas as pl
from jax.experimental.pallas import tpu as pltpu
from jax.sharding import PartitionSpec as P

SLAB = 16
ROWS = 64
WIDTH = 1024
LANES = 128
BLOCKS = WIDTH // LANES
DEPTH = 64
TILES = 8
HALO = 8
SMEM = pl.BlockSpec(memory_space=pltpu.SMEM)
VMEM = pl.BlockSpec(memory_space=pltpu.VMEM)
LIMIT = 48 * 1024 * 1024


def lane_index(rows):
    return lax.broadcasted_iota(jnp.int32, (rows, LANES), 1)


def column_lerp(plane, rel, near, far):
    rows = plane.shape[0]
    lane = lane_index(rows)
    keep_near = lane >= rel
    keep_far = lane >= rel + 1
    last_near = jnp.zeros((rows, LANES), jnp.float32)
    last_far = last_near
    out = []
    for j in range(BLOCKS):
        block = plane[:, j * LANES : (j + 1) * LANES]
        turn_near = pltpu.roll(block, rel, 1)
        turn_far = pltpu.roll(block, rel + 1, 1)
        out.append(
            near * jnp.where(keep_near, turn_near, last_near)
            + far * jnp.where(keep_far, turn_far, last_far)
        )
        last_near, last_far = turn_near, turn_far
    return out


def shift_columns(blocks, distance):
    rows = blocks[0].shape[0]
    part = distance & (LANES - 1)
    whole = jnp.full((rows, LANES), distance >> 7, jnp.int32) == 1
    own = lane_index(rows) >= part
    zero = jnp.zeros_like(blocks[0])
    turned = [pltpu.roll(block, part, 1) for block in blocks]
    placed = [jnp.where(whole, turned[j - 1] if j else zero, turned[j]) for j in range(BLOCKS)]
    return [jnp.where(own, placed[j], placed[j - 1] if j else zero) for j in range(BLOCKS)]


def column_terms(shear_ref, depth_pos, base):
    num = shear_ref[0] * depth_pos
    far = (num & 31).astype(jnp.float32) * (1.0 / 32.0)
    return (num >> 5) - base, 1.0 - far, far


def row_terms(shear_ref, depth_pos, base):
    num = shear_ref[1] * depth_pos
    far = (num & 127).astype(jnp.float32) * (1.0 / 128.0)
    return (num >> 7) - base, 1.0 - far, far


def march_rows(first, depth_idx, shear_ref, sigma, lines, stage, stage_row):
    row_base = (shear_ref[1] * depth_idx) >> 3
    total = [jnp.zeros((8, LANES), jnp.float32) for _ in range(BLOCKS)]
    light = [jnp.zeros((8, LANES), jnp.float32) for _ in range(BLOCKS)]
    trans = [jnp.ones((8, LANES), jnp.float32) for _ in range(BLOCKS)]
    for i in range(SLAB):
        rel, near, far = row_terms(shear_ref, depth_idx * SLAB + i, row_base)
        near = near * -sigma
        far = far * -sigma
        start = first + HALO - rel
        for j in range(BLOCKS):
            step = near * lines[i, j, pl.ds(start, 8), :] + far * lines[i, j, pl.ds(start - 1, 8), :]
            total[j] = total[j] + step
            after = jnp.exp2(total[j])
            light[j] = light[j] + step * (trans[j] - after)
            trans[j] = after
    col_base = (shear_ref[0] * depth_idx) >> 1
    scale = -1.0 / jnp.full((8, LANES), sigma, jnp.float32)
    total = shift_columns(total, col_base)
    light = shift_columns([scale * value for value in light], col_base)
    for j in range(BLOCKS):
        stage[pl.ds(stage_row * 16 + j, 8, stride=16), :] = total[j]
        stage[pl.ds(stage_row * 16 + 8 + j, 8, stride=16), :] = light[j]


def bulk_kernel(shear_ref, ext_ref, empty_ref, volume_ref, out_ref, lines, stage):
    depth_idx = lax.axis_index("depth")
    tile_pos = lax.axis_index("tile")
    sigma = ext_ref[0] * (4.0 / 1024.0 * math.log2(math.e))
    own_count = empty_ref[0, tile_pos]
    col_base = (shear_ref[0] * depth_idx) >> 1

    @pl.loop(0, SLAB)
    def _(i):
        rel, near, far = column_terms(shear_ref, depth_idx * SLAB + i, col_base)
        live = (i >= own_count).astype(jnp.float32)
        for c in range(ROWS // 16):
            plane = volume_ref[i, c * 16 : (c + 1) * 16, :].astype(jnp.float32)
            blocks = column_lerp(plane, rel, near * live, far * live)
            for j in range(BLOCKS):
                lines[i, j, HALO + c * 16 : HALO + (c + 1) * 16, :] = blocks[j]

    @pl.loop(1, ROWS // 8)
    def _(c):
        march_rows(c * 8, depth_idx, shear_ref, sigma, lines, stage, c * 8)

    row_base = (shear_ref[1] * depth_idx) >> 3

    @pl.loop(8, ROWS)
    def _(r):
        out_ref[(row_base + r) & (ROWS - 1)] = stage[pl.ds(r * 16, 16), :]


def edge_kernel(shear_ref, ext_ref, empty_ref, volume_ref, above_ref, bulk_ref, out_ref, lines, stage):
    depth_idx = lax.axis_index("depth")
    tile_pos = lax.axis_index("tile")
    sigma = ext_ref[0] * (4.0 / 1024.0 * math.log2(math.e))
    own_count = empty_ref[0, tile_pos]
    above_count = empty_ref[0, jnp.maximum(tile_pos - 1, 0)]
    col_base = (shear_ref[0] * depth_idx) >> 1
    row_base = (shear_ref[1] * depth_idx) >> 3
    out_ref[...] = bulk_ref[...]

    @pl.loop(0, SLAB)
    def _(i):
        rel, near, far = column_terms(shear_ref, depth_idx * SLAB + i, col_base)
        live = (i >= own_count).astype(jnp.float32)
        plane = volume_ref[i].astype(jnp.float32)[:8]
        blocks = column_lerp(plane, rel, near * live, far * live)
        live = (i >= above_count).astype(jnp.float32)
        plane = above_ref[i].astype(jnp.float32)[8:]
        halos = column_lerp(plane, rel, near * live, far * live)
        for j in range(BLOCKS):
            lines[i, j, HALO : HALO + 8, :] = blocks[j]
            lines[i, j, 0:HALO, :] = halos[j]

    march_rows(0, depth_idx, shear_ref, sigma, lines, stage, 0)
    for r in range(8):
        out_ref[(row_base + r) & (ROWS - 1)] = stage[r * 16 : (r + 1) * 16, :]


def compose_kernel(shear_ref, parts_ref, front_ref, back_ref):
    row = lax.axis_index("depth")

    def run(want_back):
        total = jnp.zeros((8, LANES), jnp.float32)
        light = jnp.zeros((8, LANES), jnp.float32)
        for d in range(DEPTH):
            is_back = ((shear_ref[1] * d) >> 3) > row
            use = jnp.where(is_back, jnp.float32(want_back), jnp.float32(1 - want_back))
            light = light + (use * jnp.exp2(total)) * parts_ref[d, 8:16, :]
            total = total + use * parts_ref[d, 0:8, :]
        return total, light

    front_ref[0:8, :], front_ref[8:16, :] = run(0)
    back_ref[0:8, :], back_ref[8:16, :] = run(1)


def spread_kernel(front_ref, back_ref, out_ref):
    total = front_ref[0:8, :] + back_ref[0:8, :]
    light = front_ref[8:16, :] + jnp.exp2(front_ref[0:8, :]) * back_ref[8:16, :]
    for p in range(DEPTH):
        out_ref[p, 0:8, :] = total
        out_ref[p, 8:16, :] = light


def image_kernel(palette_ref, whole_ref, image_ref):
    @pl.loop(0, ROWS // 8)
    def _(c):
        rows = pl.ds(pl.multiple_of(c * 8, 8), 8)
        for j in range(BLOCKS):
            columns = slice(j * LANES, (j + 1) * LANES)
            opacity = 1.0 - jnp.exp2(whole_ref[pl.ds(c * 128 + j, 8, stride=16), :])
            light = whole_ref[pl.ds(c * 128 + 8 + j, 8, stride=16), :]
            for k in range(3):
                image_ref[k, rows, columns] = palette_ref[0, k] * opacity + palette_ref[1, k] * light
            image_ref[3, rows, columns] = opacity


def call(kernel, out_shape, in_specs, scratch=()):
    return pl.pallas_call(
        kernel,
        out_shape=out_shape,
        in_specs=in_specs,
        out_specs=jax.tree.map(lambda _: VMEM, out_shape),
        scratch_shapes=list(scratch),
        compiler_params=pltpu.CompilerParams(vmem_limit_bytes=LIMIT),
    )


def per_device(volume, empty_slices, shear, extinction, palette):
    f32 = jnp.float32
    parts_shape = jax.ShapeDtypeStruct((DEPTH, 16, LANES), f32)
    piece_shape = jax.ShapeDtypeStruct((16, LANES), f32)
    down = [(i, i + 1) for i in range(TILES - 1)]
    above = lax.ppermute(volume[:, ROWS - 16 :, :], "tile", down)
    bulk = call(
        bulk_kernel,
        parts_shape,
        [SMEM, SMEM, SMEM, VMEM],
        [
            pltpu.VMEM((SLAB, BLOCKS, HALO + ROWS, LANES), f32),
            pltpu.VMEM((ROWS * 16, LANES), f32),
        ],
    )(shear, extinction, empty_slices, volume)
    parts = call(
        edge_kernel,
        parts_shape,
        [SMEM, SMEM, SMEM, VMEM, VMEM, VMEM],
        [
            pltpu.VMEM((SLAB, BLOCKS, HALO + 8, LANES), f32),
            pltpu.VMEM((8 * 16, LANES), f32),
        ],
    )(shear, extinction, empty_slices, volume[:, :16, :], above, bulk)
    parts = lax.all_to_all(parts, "depth", 0, 0, tiled=True)
    front, back = call(compose_kernel, (piece_shape, piece_shape), [SMEM, VMEM])(shear, parts)
    back = lax.ppermute(back, "tile", down)
    copies = call(spread_kernel, parts_shape, [VMEM, VMEM])(front, back)
    whole = lax.all_to_all(copies, "depth", 0, 0, tiled=True)
    image_shape = jax.ShapeDtypeStruct((4, ROWS, WIDTH), f32)
    return call(image_kernel, image_shape, [SMEM, VMEM])(palette, whole.reshape(ROWS * 16, LANES))


def solution(mesh):
    in_specs = (P("depth", "tile", None), P("depth", None), P(), P(), P())
    out_specs = P(None, "tile", None)
    return jax.shard_map(
        per_device, mesh=mesh, in_specs=in_specs, out_specs=out_specs, check_vma=False
    )
```

time: 288 us -> 81.7 us (0.28)
  the two profiles are of different devices: /device:TPU:1 before, /device:TPU:193 now
where the time goes in v1:
time: 81.7 us; the launch traced here: 81.5 us
  blocking collectives  53.3 us (65%)
  starting transfers between devices  10.5 us (13%)
  Pallas kernels  9.67 us (12%)
  waiting for transfers between devices  5.82 us (7%)
  local copies, waits for them, and re-layouts  1.44 us (2%)
    all_to_all x1, blocking collectives, per_device(): parts = lax.all_to_all(parts, 'depth', 0, 0, tiled=True)  29.2 us
    all_to_all x1, blocking collectives, per_device(): whole = lax.all_to_all(copies, 'depth', 0, 0, tiled=True)  24.1 us
    ppermute x1, starting transfers between devices, per_device(): back = lax.ppermute(back, 'tile', down)  5.32 us
    ppermute x1, starting transfers between devices, per_device(): above = lax.ppermute(volume[:, ROWS - 16:, :], 'tile', down)  5.21 us
    ppermute x1, waiting for transfers between devices, per_device(): above = lax.ppermute(volume[:, ROWS - 16:, :], 'tile', down)  5.05 us
    pallas_call x1, Pallas kernels, per_device(): call(bulk_kernel, parts_shape, [SMEM, SMEM, SMEM, VMEM], [pltpu.VMEM((SLA...  4.83 us
    pallas_call x1, Pallas kernels, per_device(): call(edge_kernel, parts_shape, [SMEM, SMEM, SMEM, VMEM, VMEM, VMEM], [plt...  2.3 us
    pallas_call x1, Pallas kernels, per_device(): call(image_kernel, image_shape, [SMEM, VMEM])  1.77 us
  transfers between devices with their start and end apart: 2, of which 2 were waited for; matrix products, arithmetic and copies ran while one was open for 0% of the time, Pallas kernels for 6%

profile of v1, /device:TPU:193, one launch (start us, length us, event | category | flops | bytes accessed | tf_op | source)
XLA Modules:
  0.0 81.5 jit_solution(6238563490192184913)
XLA Ops:
  0.0 0.0 copy-start
  0.0 0.0 copy-start.2
  0.0 0.0 copy-start.1
  0.0 1.4 %fusion = (bf16[16,16,1024]{2,1,0:T(8,128)(2,1)S(1)}, bf16[16,16,1024]{2,1,0:T(8,128)(2,1)S(1)}) fusion(bf16[16,64,1024]{2,1,0:T(8,128)(2,1)} %volume_ref.1), kind=kLoop, calls=%fused_computation | loop fusion | bytes 2097152 | tf_op jit(solution)/shard_map/slice | solution.py:206
  1.4 5.2 %collective-permute-start = (bf16[16,16,1024]{2,1,0:T(8,128)(2,1)S(1)}, bf16[16,16,1024]{2,1,0:T(8,128)(2,1)S(1)}, u32[]{:S(2)}, u32[]{:S(2)}) collective-permute-start(bf16[16,16,1024]{2,1,0:T(8,128)(2,1)S(1)} %get-tuple-element.9), channel_id=1, source_target_pairs={{0,1},{1,2},{2,3},{3,4},{4,5},{5,6},{6,7},{8,9},{9,10},{10,11},{11... | collective-permute-start | bytes 1572872 | tf_op jit(solution)/shard_map/ppermute | solution.py:206
  7.3 0.0 copy-done
  7.3 0.0 copy-done.2
  7.3 0.0 copy-done.1
  7.3 4.8 %shard_map.55.bulk_ref = f32[64,16,128]{2,1,0:T(8,128)S(1)} custom-call(s32[2]{0:T(128)S(1)} %copy-done.1, f32[1]{0:T(128)S(6)} %copy.6.ext_ref, s32[1,8]{1,0:T(1,128)S(1)} %copy-done.2, bf16[16,64,1024]{2,1,0:T(8,128)(2,1)S(1)} %copy-done), custom_call_target="tpu_custom_call" | custom-call | tf_op jit(solution)/shard_map/pallas_call | solution.py:207
  12.2 5.1 %collective-permute-done.above_ref = bf16[16,16,1024]{2,1,0:T(8,128)(2,1)S(1)} collective-permute-done((bf16[16,16,1024]{2,1,0:T(8,128)(2,1)S(1)}, bf16[16,16,1024]{2,1,0:T(8,128)(2,1)S(1)}, u32[]{:S(2)}, u32[]{:S(2)}) %collective-permute-start) | collective-permute-done | bytes 524320 | tf_op jit(solution)/shard_map/ppermute | solution.py:206
  17.2 2.3 %shard_map.56 = f32[64,16,128]{2,1,0:T(8,128)S(1)} custom-call(s32[2]{0:T(128)S(1)} %copy-done.1, f32[1]{0:T(128)S(6)} %copy.6.ext_ref, s32[1,8]{1,0:T(1,128)S(1)} %copy-done.2, bf16[16,16,1024]{2,1,0:T(8,128)(2,1)S(1)} %get-tuple-element.10.volume_ref, bf16[16,16,1024]{2,1,0:T(8,128)(2,1)S(1)} %collective-permute-done.above_ref, ...), custom_call_target="tpu_custom_call" | custom-call | tf_op jit(solution)/shard_map/pallas_call | solution.py:216
  19.5 0.0 copy-start.3
  19.5 29.2 %all_to_all.10.parts_ref = f32[64,16,128]{2,1,0:T(8,128)S(1)} all-to-all(f32[64,16,128]{2,1,0:T(8,128)S(1)} %shard_map.56), channel_id=1, replica_groups=mesh['depth'=64,'tile'=8] {'depth'}, dimensions={0} | all-to-all | bytes 1048576 | tf_op jit(solution)/shard_map/all_to_all | solution.py:225
  48.7 0.7 shard_map.57
  49.5 5.3 %collective-permute-start.1 = (f32[16,128]{1,0:T(8,128)S(1)}, f32[16,128]{1,0:T(8,128)S(1)}, u32[]{:S(2)}, u32[]{:S(2)}) collective-permute-start(f32[16,128]{1,0:T(8,128)S(1)} %get-tuple-element.8), channel_id=1, source_target_pairs={{0,1},{1,2},{2,3},{3,4},{4,5},{5,6},{6,7},{8,9},{9,10},{10,11},{11... | collective-permute-start | bytes 24584 | tf_op jit(solution)/shard_map/ppermute | solution.py:227
  54.8 0.8 collective-permute-done.1.back_ref
  55.6 24.1 %all_to_all.11 = f32[64,16,128]{2,1,0:T(8,128)S(1)} all-to-all(f32[64,16,128]{2,1,0:T(8,128)S(1)} %shard_map.58), channel_id=1, replica_groups=mesh['depth'=64,'tile'=8] {'depth'}, dimensions={0} | all-to-all | bytes 1048576 | tf_op jit(solution)/shard_map/all_to_all | solution.py:229
  79.7 0.0 copy-done.3
  79.7 1.8 %shard_map.59 = f32[4,64,1024]{2,1,0:T(8,128)} custom-call(f32[2,3]{1,0:T(2,128)S(1)} %copy-done.3, f32[1024,128]{1,0:T(8,128)S(1)} %bitcast.1), custom_call_target="tpu_custom_call" | custom-call | tf_op jit(solution)/shard_map/pallas_call | solution.py:231
  (1 shorter events, 0.0 us)
Async XLA Ops:
  0.0 7.3 %copy-start = (bf16[16,64,1024]{2,1,0:T(8,128)(2,1)S(1)}, bf16[16,64,1024]{2,1,0:T(8,128)(2,1)}, u32[]{:S(2)}) copy-start(bf16[16,64,1024]{2,1,0:T(8,128)(2,1)} %volume_ref.1) | copy-start | bytes 6291460
  0.0 7.3 %copy-start.2 = (s32[1,8]{1,0:T(1,128)S(1)}, s32[1,8]{1,0:T(1,128)}, u32[]{:S(2)}) copy-start(s32[1,8]{1,0:T(1,128)} %empty_ref.3) | copy-start | bytes 100
  0.0 7.3 %copy-start.1 = (s32[2]{0:T(128)S(1)}, s32[2]{0:T(128)}, u32[]{:S(2)}) copy-start(s32[2]{0:T(128)} %shear_ref.5) | copy-start | bytes 28
  1.4 15.8 %collective-permute-start = (bf16[16,16,1024]{2,1,0:T(8,128)(2,1)S(1)}, bf16[16,16,1024]{2,1,0:T(8,128)(2,1)S(1)}, u32[]{:S(2)}, u32[]{:S(2)}) collective-permute-start(bf16[16,16,1024]{2,1,0:T(8,128)(2,1)S(1)} %get-tuple-element.9), channel_id=1, source_target_pairs={{0,1},{1,2},{2,3},{3,4},{4,5},{5,6},{6,7},{8,9},{9,10},{10,11},{11... | collective-permute-start | bytes 1572872 | tf_op jit(solution)/shard_map/ppermute | solution.py:206
  19.5 60.2 %copy-start.3 = (f32[2,3]{1,0:T(2,128)S(1)}, f32[2,3]{1,0:T(2,128)}, u32[]{:S(2)}) copy-start(f32[2,3]{1,0:T(2,128)} %palette_ref.1) | copy-start | bytes 76
  49.5 6.1 %collective-permute-start.1 = (f32[16,128]{1,0:T(8,128)S(1)}, f32[16,128]{1,0:T(8,128)S(1)}, u32[]{:S(2)}, u32[]{:S(2)}) collective-permute-start(f32[16,128]{1,0:T(8,128)S(1)} %get-tuple-element.8), channel_id=1, source_target_pairs={{0,1},{1,2},{2,3},{3,4},{4,5},{5,6},{6,7},{8,9},{9,10},{10,11},{11... | collective-permute-start | bytes 24584 | tf_op jit(solution)/shard_map/ppermute | solution.py:227

commit v2 on v1

--- a/solution.py
+++ b/solution.py
@@ -1,4 +1,3 @@
-import functools
 import math
 
 import jax
@@ -19,6 +18,43 @@
 SMEM = pl.BlockSpec(memory_space=pltpu.SMEM)
 VMEM = pl.BlockSpec(memory_space=pltpu.VMEM)
 LIMIT = 48 * 1024 * 1024
+
+
+TOP = 65535.0
+BRICK_RANGE = (-27.0, math.log2(16 * 4 / 1024 * math.log2(math.e)) + 0.001)
+IMAGE_RANGE = (-25.0, math.log2(4 * math.log2(math.e)) + 0.001)
+
+
+def to_code(value):
+    whole = (jnp.clip(value, 0.0, TOP) + 0.5).astype(jnp.int32)
+    return whole - 32768
+
+
+def from_code(code):
+    return (code.astype(jnp.int32) + 32768).astype(jnp.float32)
+
+
+def depth_to_code(depth, limits):
+    low, high = limits
+    steps = (TOP - 1.0) / (high - low)
+    seen = depth >= 2.0**low
+    level = (jnp.log2(jnp.where(seen, depth, 1.0)) - low) * steps + 1.0
+    return to_code(jnp.where(seen, level, 0.0))
+
+
+def depth_from_code(code, limits):
+    low, high = limits
+    level = from_code(code)
+    depth = jnp.exp2((level - 1.0) * ((high - low) / (TOP - 1.0)) + low)
+    return jnp.where(level > 0.5, depth, 0.0)
+
+
+def encode_brick(total, light):
+    depth = -total
+    seen = depth >= 2.0 ** BRICK_RANGE[0]
+    mean = light / (jnp.where(seen, depth, 1.0) * math.log(2.0))
+    codes = [depth_to_code(depth, BRICK_RANGE), to_code(jnp.where(seen, mean * TOP, 0.0))]
+    return jnp.concatenate(codes, axis=0).astype(jnp.int16)
 
 
 def lane_index(rows):
@@ -118,7 +154,8 @@
 
     @pl.loop(8, ROWS)
     def _(r):
-        out_ref[(row_base + r) & (ROWS - 1)] = stage[pl.ds(r * 16, 16), :]
+        piece = stage[pl.ds(r * 16, 16), :]
+        out_ref[(row_base + r) & (ROWS - 1)] = encode_brick(piece[:8], piece[8:])
 
 
 def edge_kernel(shear_ref, ext_ref, empty_ref, volume_ref, above_ref, bulk_ref, out_ref, lines, stage):
@@ -130,58 +167,65 @@
     col_base = (shear_ref[0] * depth_idx) >> 1
     row_base = (shear_ref[1] * depth_idx) >> 3
     out_ref[...] = bulk_ref[...]
-
-    @pl.loop(0, SLAB)
-    def _(i):
+    above = above_ref[...].astype(jnp.float32)
+    for i in range(SLAB):
         rel, near, far = column_terms(shear_ref, depth_idx * SLAB + i, col_base)
         live = (i >= own_count).astype(jnp.float32)
-        plane = volume_ref[i].astype(jnp.float32)[:8]
+        plane = volume_ref[i, :16, :].astype(jnp.float32)[:8]
         blocks = column_lerp(plane, rel, near * live, far * live)
         live = (i >= above_count).astype(jnp.float32)
-        plane = above_ref[i].astype(jnp.float32)[8:]
-        halos = column_lerp(plane, rel, near * live, far * live)
+        halos = column_lerp(above[2 * i : 2 * i + 2], rel, near * live, far * live)
         for j in range(BLOCKS):
             lines[i, j, HALO : HALO + 8, :] = blocks[j]
-            lines[i, j, 0:HALO, :] = halos[j]
+            lines[i, j, HALO - 2 : HALO, :] = halos[j]
 
     march_rows(0, depth_idx, shear_ref, sigma, lines, stage, 0)
     for r in range(8):
-        out_ref[(row_base + r) & (ROWS - 1)] = stage[r * 16 : (r + 1) * 16, :]
+        piece = stage[r * 16 : (r + 1) * 16, :]
+        out_ref[(row_base + r) & (ROWS - 1)] = encode_brick(piece[:8], piece[8:])
 
 
 def compose_kernel(shear_ref, parts_ref, front_ref, back_ref):
     row = lax.axis_index("depth")
-
-    def run(want_back):
-        total = jnp.zeros((8, LANES), jnp.float32)
-        light = jnp.zeros((8, LANES), jnp.float32)
-        for d in range(DEPTH):
-            is_back = ((shear_ref[1] * d) >> 3) > row
-            use = jnp.where(is_back, jnp.float32(want_back), jnp.float32(1 - want_back))
-            light = light + (use * jnp.exp2(total)) * parts_ref[d, 8:16, :]
-            total = total + use * parts_ref[d, 0:8, :]
-        return total, light
-
-    front_ref[0:8, :], front_ref[8:16, :] = run(0)
-    back_ref[0:8, :], back_ref[8:16, :] = run(1)
+    zero = jnp.zeros((8, LANES), jnp.float32)
+    totals = [zero, zero]
+    lights = [zero, zero]
+    for d in range(DEPTH):
+        codes = parts_ref[d].astype(jnp.int32)
+        depth = depth_from_code(codes[:8], BRICK_RANGE)
+        light = from_code(codes[8:]) * (math.log(2.0) / TOP) * depth
+        is_back = (((shear_ref[1] * d) >> 3) > row).astype(jnp.float32)
+        for side, use in enumerate((1.0 - is_back, is_back)):
+            lights[side] = lights[side] + (use * jnp.exp2(-totals[side])) * light
+            totals[side] = totals[side] + use * depth
+    front_ref[0:8, :], front_ref[8:16, :] = totals[0], lights[0]
+    back_ref[0:8, :], back_ref[8:16, :] = totals[1], lights[1]
 
 
 def spread_kernel(front_ref, back_ref, out_ref):
-    total = front_ref[0:8, :] + back_ref[0:8, :]
-    light = front_ref[8:16, :] + jnp.exp2(front_ref[0:8, :]) * back_ref[8:16, :]
+    depth = front_ref[0:8, :] + back_ref[0:8, :]
+    light = front_ref[8:16, :] + jnp.exp2(-front_ref[0:8, :]) * back_ref[8:16, :]
+    opacity = 1.0 - jnp.exp2(-depth)
+    mean = light / jnp.maximum(opacity, 2.0 ** IMAGE_RANGE[0])
+    codes = jnp.concatenate([depth_to_code(depth, IMAGE_RANGE), to_code(mean * TOP)], axis=0)
+    codes = codes.astype(jnp.int16)
     for p in range(DEPTH):
-        out_ref[p, 0:8, :] = total
-        out_ref[p, 8:16, :] = light
-
-
-def image_kernel(palette_ref, whole_ref, image_ref):
+        out_ref[p] = codes
+
+
+def image_kernel(palette_ref, whole_ref, image_ref, stage):
     @pl.loop(0, ROWS // 8)
     def _(c):
+        for r in range(8):
+            codes = whole_ref[c * 8 + r].astype(jnp.int32)
+            opacity = 1.0 - jnp.exp2(-depth_from_code(codes[:8], IMAGE_RANGE))
+            stage[r * 16 : r * 16 + 8, :] = opacity
+            stage[r * 16 + 8 : r * 16 + 16, :] = from_code(codes[8:]) * (1.0 / TOP) * opacity
         rows = pl.ds(pl.multiple_of(c * 8, 8), 8)
         for j in range(BLOCKS):
             columns = slice(j * LANES, (j + 1) * LANES)
-            opacity = 1.0 - jnp.exp2(whole_ref[pl.ds(c * 128 + j, 8, stride=16), :])
-            light = whole_ref[pl.ds(c * 128 + 8 + j, 8, stride=16), :]
+            opacity = stage[pl.ds(j, 8, stride=16), :]
+            light = stage[pl.ds(8 + j, 8, stride=16), :]
             for k in range(3):
                 image_ref[k, rows, columns] = palette_ref[0, k] * opacity + palette_ref[1, k] * light
             image_ref[3, rows, columns] = opacity
@@ -200,10 +244,10 @@
 
 def per_device(volume, empty_slices, shear, extinction, palette):
     f32 = jnp.float32
-    parts_shape = jax.ShapeDtypeStruct((DEPTH, 16, LANES), f32)
+    parts_shape = jax.ShapeDtypeStruct((DEPTH, 16, LANES), jnp.int16)
     piece_shape = jax.ShapeDtypeStruct((16, LANES), f32)
     down = [(i, i + 1) for i in range(TILES - 1)]
-    above = lax.ppermute(volume[:, ROWS - 16 :, :], "tile", down)
+    above = lax.ppermute(volume[:, ROWS - 2 :, :].reshape(2 * SLAB, WIDTH), "tile", down)
     bulk = call(
         bulk_kernel,
         parts_shape,
@@ -221,14 +265,16 @@
             pltpu.VMEM((SLAB, BLOCKS, HALO + 8, LANES), f32),
             pltpu.VMEM((8 * 16, LANES), f32),
         ],
-    )(shear, extinction, empty_slices, volume[:, :16, :], above, bulk)
+    )(shear, extinction, empty_slices, volume, above, bulk)
     parts = lax.all_to_all(parts, "depth", 0, 0, tiled=True)
     front, back = call(compose_kernel, (piece_shape, piece_shape), [SMEM, VMEM])(shear, parts)
     back = lax.ppermute(back, "tile", down)
     copies = call(spread_kernel, parts_shape, [VMEM, VMEM])(front, back)
     whole = lax.all_to_all(copies, "depth", 0, 0, tiled=True)
     image_shape = jax.ShapeDtypeStruct((4, ROWS, WIDTH), f32)
-    return call(image_kernel, image_shape, [SMEM, VMEM])(palette, whole.reshape(ROWS * 16, LANES))
+    return call(image_kernel, image_shape, [SMEM, VMEM], [pltpu.VMEM((8 * 16, LANES), f32)])(
+        palette, whole
+    )
 
 
 def solution(mesh):

time: 81.7 us -> 67.2 us (0.82)
  the two profiles are of different devices: /device:TPU:193 before, /device:TPU:1 now
where the time goes in v2:
time: 67.2 us; the launch traced here: 66.5 us
  blocking collectives  42.6 us (63%)
  Pallas kernels  9.65 us (14%)
  starting transfers between devices  8.82 us (13%)
  local copies, waits for them, and re-layouts  3.95 us (6%)
  waiting for transfers between devices  0.78 us (1%)
  between operations  0.72 us (1%)
    all_to_all x1, blocking collectives, per_device(): parts = lax.all_to_all(parts, 'depth', 0, 0, tiled=True)  24 us
    all_to_all x1, blocking collectives, per_device(): whole = lax.all_to_all(copies, 'depth', 0, 0, tiled=True)  18.5 us
    pallas_call x1, Pallas kernels, per_device(): call(bulk_kernel, parts_shape, [SMEM, SMEM, SMEM, VMEM], [pltpu.VMEM((SLA...  5.57 us
    ppermute x1, starting transfers between devices, per_device(): lax.ppermute(volume[:, ROWS - 2:, :].reshape(2 * SLAB, WIDTH), 'tile', down)  4.83 us
    ppermute x1, starting transfers between devices, per_device(): back = lax.ppermute(back, 'tile', down)  3.99 us
    unnamed x8, local copies, waits for them, and re-layouts  2.9 us
    pallas_call x1, Pallas kernels, per_device(): call(image_kernel, image_shape, [SMEM, VMEM], [pltpu.VMEM((8 * 16, LANES)...  1.97 us
  transfers between devices with their start and end apart: 2, of which 1 were waited for; matrix products, arithmetic and copies ran while one was open for 0% of the time, Pallas kernels for 8%

profile of v2, /device:TPU:1, one launch (start us, length us, event | category | flops | bytes accessed | tf_op | source)
XLA Modules:
  0.0 66.5 jit_solution(4428110618600886463)
XLA Ops:
  0.0 1.0 %slice.3 = bf16[16,2,1024]{2,1,0:T(2,128)(2,1)S(1)} slice(bf16[16,64,1024]{2,1,0:T(8,128)(2,1)} %volume_ref.3), slice={[0:16], [62:64], [0:1024]} | slice | bytes 131072 | tf_op jit(solution)/shard_map/slice | solution.py:250
  1.1 4.8 %collective-permute-start = (bf16[32,1024]{1,0:T(8,128)(2,1)S(1)}, bf16[32,1024]{1,0:T(8,128)(2,1)S(1)}, u32[]{:S(2)}, u32[]{:S(2)}) collective-permute-start(bf16[32,1024]{1,0:T(8,128)(2,1)S(1)} %reshape.3), channel_id=1, source_target_pairs={{0,1},{1,2},{2,3},{3,4},{4,5},{5,6},{6,7},{8,9},{9,10},{10,11},{11... | collective-permute-start | bytes 196616 | tf_op jit(solution)/shard_map/ppermute | solution.py:250
  6.5 0.0 copy-start
  6.6 1.6 %copy-done = bf16[16,64,1024]{2,1,0:T(8,128)(2,1)S(1)} copy-done((bf16[16,64,1024]{2,1,0:T(8,128)(2,1)S(1)}, bf16[16,64,1024]{2,1,0:T(8,128)(2,1)}, u32[]{:S(2)}) %copy-start) | copy-done | bytes 2097176
  8.1 0.0 copy-start.1
  8.1 0.7 copy-done.1
  8.8 0.0 copy-start.2
  8.8 0.7 copy-done.2
  9.4 5.6 %shard_map.55.bulk_ref = s16[64,16,128]{2,1,0:T(8,128)(2,1)S(1)} custom-call(s32[2]{0:T(128)S(1)} %copy-done.1, f32[1]{0:T(128)S(6)} %copy.6.ext_ref, s32[1,8]{1,0:T(1,128)S(1)} %copy-done.2, bf16[16,64,1024]{2,1,0:T(8,128)(2,1)S(1)} %copy-done), custom_call_target="tpu_custom_call" | custom-call | tf_op jit(solution)/shard_map/pallas_call | solution.py:251
  15.0 0.0 copy-start.3
  15.0 0.0 collective-permute-done.above_ref
  15.1 1.2 %shard_map.56 = s16[64,16,128]{2,1,0:T(8,128)(2,1)S(1)} custom-call(s32[2]{0:T(128)S(1)} %copy-done.1, f32[1]{0:T(128)S(6)} %copy.6.ext_ref, s32[1,8]{1,0:T(1,128)S(1)} %copy-done.2, bf16[16,64,1024]{2,1,0:T(8,128)(2,1)S(1)} %copy-done, bf16[32,1024]{1,0:T(8,128)(2,1)S(1)} %collective-permute-done.above_ref, s16[64,16,128]{2,1,0:T(8,128)(2,1)S(1)} %shard_map.55.bulk_ref), custom_call_target="tpu_custom_call" | custom-call | tf_op jit(solution)/shard_map/pallas_call | solution.py:260
  16.3 24.0 %all_to_all.10.parts_ref = s16[64,16,128]{2,1,0:T(8,128)(2,1)S(1)} all-to-all(s16[64,16,128]{2,1,0:T(8,128)(2,1)S(1)} %shard_map.56), channel_id=1, replica_groups=mesh['depth'=64,'tile'=8] {'depth'}, dimensions={0} | all-to-all | bytes 524288 | tf_op jit(solution)/shard_map/all_to_all | solution.py:269
  40.3 0.9 %shard_map.57 = (f32[16,128]{1,0:T(8,128)S(1)}, f32[16,128]{1,0:T(8,128)S(1)}) custom-call(s32[2]{0:T(128)S(1)} %copy-done.1, s16[64,16,128]{2,1,0:T(8,128)(2,1)S(1)} %all_to_all.10.parts_ref), custom_call_target="tpu_custom_call" | custom-call | tf_op jit(solution)/shard_map/pallas_call | solution.py:270
  41.2 4.0 %collective-permute-start.1 = (f32[16,128]{1,0:T(8,128)S(1)}, f32[16,128]{1,0:T(8,128)S(1)}, u32[]{:S(2)}, u32[]{:S(2)}) collective-permute-start(f32[16,128]{1,0:T(8,128)S(1)} %get-tuple-element.8), channel_id=1, source_target_pairs={{0,1},{1,2},{2,3},{3,4},{4,5},{5,6},{6,7},{8,9},{9,10},{10,11},{11... | collective-permute-start | bytes 24584 | tf_op jit(solution)/shard_map/ppermute | solution.py:271
  45.2 0.8 %collective-permute-done.1.back_ref = f32[16,128]{1,0:T(8,128)S(1)} collective-permute-done((f32[16,128]{1,0:T(8,128)S(1)}, f32[16,128]{1,0:T(8,128)S(1)}, u32[]{:S(2)}, u32[]{:S(2)}) %collective-permute-start.1) | collective-permute-done | bytes 8224 | tf_op jit(solution)/shard_map/ppermute | solution.py:271
  45.9 0.1 shard_map.58
  46.0 18.5 %all_to_all.11.whole_ref = s16[64,16,128]{2,1,0:T(8,128)(2,1)S(1)} all-to-all(s16[64,16,128]{2,1,0:T(8,128)(2,1)S(1)} %shard_map.58), channel_id=1, replica_groups=mesh['depth'=64,'tile'=8] {'depth'}, dimensions={0} | all-to-all | bytes 524288 | tf_op jit(solution)/shard_map/all_to_all | solution.py:273
  64.5 0.0 copy-done.3
  64.5 2.0 %shard_map.59 = f32[4,64,1024]{2,1,0:T(8,128)} custom-call(f32[2,3]{1,0:T(2,128)S(1)} %copy-done.3, s16[64,16,128]{2,1,0:T(8,128)(2,1)S(1)} %all_to_all.11.whole_ref), custom_call_target="tpu_custom_call" | custom-call | tf_op jit(solution)/shard_map/pallas_call | solution.py:275
  (1 shorter events, 0.0 us)
Async XLA Ops:
  1.1 14.0 %collective-permute-start = (bf16[32,1024]{1,0:T(8,128)(2,1)S(1)}, bf16[32,1024]{1,0:T(8,128)(2,1)S(1)}, u32[]{:S(2)}, u32[]{:S(2)}) collective-permute-start(bf16[32,1024]{1,0:T(8,128)(2,1)S(1)} %reshape.3), channel_id=1, source_target_pairs={{0,1},{1,2},{2,3},{3,4},{4,5},{5,6},{6,7},{8,9},{9,10},{10,11},{11... | collective-permute-start | bytes 196616 | tf_op jit(solution)/shard_map/ppermute | solution.py:250
  6.5 1.6 %copy-start = (bf16[16,64,1024]{2,1,0:T(8,128)(2,1)S(1)}, bf16[16,64,1024]{2,1,0:T(8,128)(2,1)}, u32[]{:S(2)}) copy-start(bf16[16,64,1024]{2,1,0:T(8,128)(2,1)} %volume_ref.3) | copy-start | bytes 6291460
  8.1 0.7 copy-start.1
  8.8 0.7 copy-start.2
  15.0 49.5 %copy-start.3 = (f32[2,3]{1,0:T(2,128)S(1)}, f32[2,3]{1,0:T(2,128)}, u32[]{:S(2)}) copy-start(f32[2,3]{1,0:T(2,128)} %palette_ref.1) | copy-start | bytes 76
  41.2 4.8 %collective-permute-start.1 = (f32[16,128]{1,0:T(8,128)S(1)}, f32[16,128]{1,0:T(8,128)S(1)}, u32[]{:S(2)}, u32[]{:S(2)}) collective-permute-start(f32[16,128]{1,0:T(8,128)S(1)} %get-tuple-element.8), channel_id=1, source_target_pairs={{0,1},{1,2},{2,3},{3,4},{4,5},{5,6},{6,7},{8,9},{9,10},{10,11},{11... | collective-permute-start | bytes 24584 | tf_op jit(solution)/shard_map/ppermute | solution.py:271

commit v3 on v2

--- a/solution.py
+++ b/solution.py
@@ -152,10 +152,11 @@
 
     row_base = (shear_ref[1] * depth_idx) >> 3
 
-    @pl.loop(8, ROWS)
-    def _(r):
-        piece = stage[pl.ds(r * 16, 16), :]
-        out_ref[(row_base + r) & (ROWS - 1)] = encode_brick(piece[:8], piece[8:])
+    @pl.loop(8, ROWS, step=8)
+    def _(first):
+        for r in range(8):
+            piece = stage[pl.ds((first + r) * 16, 16), :]
+            out_ref[(row_base + first + r) & (ROWS - 1)] = encode_brick(piece[:8], piece[8:])
 
 
 def edge_kernel(shear_ref, ext_ref, empty_ref, volume_ref, above_ref, bulk_ref, out_ref, lines, stage):
@@ -171,7 +172,7 @@
     for i in range(SLAB):
         rel, near, far = column_terms(shear_ref, depth_idx * SLAB + i, col_base)
         live = (i >= own_count).astype(jnp.float32)
-        plane = volume_ref[i, :16, :].astype(jnp.float32)[:8]
+        plane = volume_ref[i].astype(jnp.float32)[:8]
         blocks = column_lerp(plane, rel, near * live, far * live)
         live = (i >= above_count).astype(jnp.float32)
         halos = column_lerp(above[2 * i : 2 * i + 2], rel, near * live, far * live)
@@ -213,30 +214,40 @@
         out_ref[p] = codes
 
 
-def image_kernel(palette_ref, whole_ref, image_ref, stage):
-    @pl.loop(0, ROWS // 8)
-    def _(c):
-        for r in range(8):
-            codes = whole_ref[c * 8 + r].astype(jnp.int32)
+def image_kernel(palette_ref, whole_ref, image_hbm, stage, image, sems):
+    base = [palette_ref[0, k] for k in range(3)]
+    slope = [palette_ref[1, k] for k in range(3)]
+    copies = []
+    for c in range(ROWS // 8):
+        rows = slice(c * 8, (c + 1) * 8)
+        for r in range(c * 8, c * 8 + 8):
+            codes = whole_ref[r].astype(jnp.int32)
             opacity = 1.0 - jnp.exp2(-depth_from_code(codes[:8], IMAGE_RANGE))
             stage[r * 16 : r * 16 + 8, :] = opacity
             stage[r * 16 + 8 : r * 16 + 16, :] = from_code(codes[8:]) * (1.0 / TOP) * opacity
-        rows = pl.ds(pl.multiple_of(c * 8, 8), 8)
         for j in range(BLOCKS):
             columns = slice(j * LANES, (j + 1) * LANES)
-            opacity = stage[pl.ds(j, 8, stride=16), :]
-            light = stage[pl.ds(8 + j, 8, stride=16), :]
+            opacity = stage[pl.ds(c * 128 + j, 8, stride=16), :]
+            light = stage[pl.ds(c * 128 + 8 + j, 8, stride=16), :]
             for k in range(3):
-                image_ref[k, rows, columns] = palette_ref[0, k] * opacity + palette_ref[1, k] * light
-            image_ref[3, rows, columns] = opacity
-
-
-def call(kernel, out_shape, in_specs, scratch=()):
+                image[k, rows, columns] = base[k] * opacity + slope[k] * light
+            image[3, rows, columns] = opacity
+        if c % 2:
+            part = pl.ds(c * 8 - 8, 16)
+            copies.append(
+                pltpu.make_async_copy(image.at[:, part], image_hbm.at[:, part], sems.at[c // 2])
+            )
+            copies[-1].start()
+    for copy in copies:
+        copy.wait()
+
+
+def call(kernel, out_shape, in_specs, scratch=(), out_specs=None):
     return pl.pallas_call(
         kernel,
         out_shape=out_shape,
         in_specs=in_specs,
-        out_specs=jax.tree.map(lambda _: VMEM, out_shape),
+        out_specs=out_specs or jax.tree.map(lambda _: VMEM, out_shape),
         scratch_shapes=list(scratch),
         compiler_params=pltpu.CompilerParams(vmem_limit_bytes=LIMIT),
     )
@@ -247,7 +258,8 @@
     parts_shape = jax.ShapeDtypeStruct((DEPTH, 16, LANES), jnp.int16)
     piece_shape = jax.ShapeDtypeStruct((16, LANES), f32)
     down = [(i, i + 1) for i in range(TILES - 1)]
-    above = lax.ppermute(volume[:, ROWS - 2 :, :].reshape(2 * SLAB, WIDTH), "tile", down)
+    first, last = lax.optimization_barrier((volume[:, :16, :], volume[:, ROWS - 16 :, :]))
+    above = lax.ppermute(last[:, 14:, :].reshape(2 * SLAB, WIDTH), "tile", down)
     bulk = call(
         bulk_kernel,
         parts_shape,
@@ -265,16 +277,24 @@
             pltpu.VMEM((SLAB, BLOCKS, HALO + 8, LANES), f32),
             pltpu.VMEM((8 * 16, LANES), f32),
         ],
-    )(shear, extinction, empty_slices, volume, above, bulk)
+    )(shear, extinction, empty_slices, first, above, bulk)
     parts = lax.all_to_all(parts, "depth", 0, 0, tiled=True)
     front, back = call(compose_kernel, (piece_shape, piece_shape), [SMEM, VMEM])(shear, parts)
     back = lax.ppermute(back, "tile", down)
     copies = call(spread_kernel, parts_shape, [VMEM, VMEM])(front, back)
     whole = lax.all_to_all(copies, "depth", 0, 0, tiled=True)
     image_shape = jax.ShapeDtypeStruct((4, ROWS, WIDTH), f32)
-    return call(image_kernel, image_shape, [SMEM, VMEM], [pltpu.VMEM((8 * 16, LANES), f32)])(
-        palette, whole
-    )
+    return call(
+        image_kernel,
+        image_shape,
+        [SMEM, VMEM],
+        [
+            pltpu.VMEM((ROWS * 16, LANES), f32),
+            pltpu.VMEM((4, ROWS, WIDTH), f32),
+            pltpu.SemaphoreType.DMA((ROWS // 16,)),
+        ],
+        pl.BlockSpec(memory_space=pl.ANY),
+    )(palette, whole)
 
 
 def solution(mesh):

time: 67.2 us -> 63.6 us (0.946)
  local copies, waits for them, and re-layouts: 3.95 us -> 1.55 us
  Pallas kernels: 9.65 us -> 8.5 us
    unnamed x8, local copies, waits for them, and re-layouts: 2.9 us -> 0.02 us
    pallas_call x1, Pallas kernels: 5.57 us -> 4.73 us  [per_device(): call(bulk_kernel, parts_shape, [SMEM, SMEM, SMEM, VMEM], [pltpu.VMEM((SLA...]
    slice x1 -> x2, local copies, waits for them, and re-layouts: 1.02 us -> 1.5 us  [the longest x1 1.43 us: per_device(): volume[:, ROWS - 16:, :]]
where the time goes in v3:
time: 63.6 us; the launch traced here: 63 us
  blocking collectives  42.6 us (67%)
  starting transfers between devices  8.82 us (14%)
  Pallas kernels  8.5 us (13%)
  local copies, waits for them, and re-layouts  1.55 us (2%)
  waiting for transfers between devices  0.78 us (1%)
  between operations  0.75 us (1%)
    all_to_all x1, blocking collectives, per_device(): parts = lax.all_to_all(parts, 'depth', 0, 0, tiled=True)  24 us
    all_to_all x1, blocking collectives, per_device(): whole = lax.all_to_all(copies, 'depth', 0, 0, tiled=True)  18.5 us
    ppermute x1, starting transfers between devices, per_device(): above = lax.ppermute(last[:, 14:, :].reshape(2 * SLAB, WIDTH), 'tile', down)  4.83 us
    pallas_call x1, Pallas kernels, per_device(): call(bulk_kernel, parts_shape, [SMEM, SMEM, SMEM, VMEM], [pltpu.VMEM((SLA...  4.73 us
    ppermute x1, starting transfers between devices, per_device(): back = lax.ppermute(back, 'tile', down)  3.99 us
    pallas_call x1, Pallas kernels, per_device(): call(image_kernel, image_shape, [SMEM, VMEM], [pltpu.VMEM((ROWS * 16, LAN...  1.65 us
    slice x1, local copies, waits for them, and re-layouts, per_device(): volume[:, ROWS - 16:, :]  1.43 us
  transfers between devices with their start and end apart: 2, of which 1 were waited for; matrix products, arithmetic and copies ran while one was open for 0% of the time, Pallas kernels for 8%

profile of v3, /device:TPU:1, one launch (start us, length us, event | category | flops | bytes accessed | tf_op | source)
XLA Modules:
  0.0 63.0 jit_solution(3959580974809953503)
XLA Ops:
  0.0 0.0 copy-start
  0.0 0.0 copy-start.2
  0.0 0.0 copy-start.1
  0.0 1.4 %fusion = (bf16[16,16,1024]{2,1,0:T(8,128)(2,1)S(1)}, bf16[16,16,1024]{2,1,0:T(8,128)(2,1)S(1)}) fusion(bf16[16,64,1024]{2,1,0:T(8,128)(2,1)} %volume_ref.1), kind=kLoop, calls=%fused_computation | loop fusion | bytes 2097152 | tf_op jit(solution)/shard_map/slice | solution.py:261
  1.4 0.1 slice.11
  1.6 4.8 %collective-permute-start = (bf16[32,1024]{1,0:T(8,128)(2,1)S(1)}, bf16[32,1024]{1,0:T(8,128)(2,1)S(1)}, u32[]{:S(2)}, u32[]{:S(2)}) collective-permute-start(bf16[32,1024]{1,0:T(8,128)(2,1)S(1)} %reshape.3), channel_id=1, source_target_pairs={{0,1},{1,2},{2,3},{3,4},{4,5},{5,6},{6,7},{8,9},{9,10},{10,11},{11... | collective-permute-start | bytes 196616 | tf_op jit(solution)/shard_map/ppermute | solution.py:262
  7.0 0.0 copy-done
  7.1 0.0 copy-done.2
  7.1 0.0 copy-done.1
  7.1 0.0 copy-start.3
  7.1 4.7 %shard_map.55.bulk_ref = s16[64,16,128]{2,1,0:T(8,128)(2,1)S(1)} custom-call(s32[2]{0:T(128)S(1)} %copy-done.1, f32[1]{0:T(128)S(6)} %copy.6.ext_ref, s32[1,8]{1,0:T(1,128)S(1)} %copy-done.2, bf16[16,64,1024]{2,1,0:T(8,128)(2,1)S(1)} %copy-done), custom_call_target="tpu_custom_call" | custom-call | tf_op jit(solution)/shard_map/pallas_call | solution.py:263
  11.8 0.0 collective-permute-done.above_ref
  11.8 1.2 %shard_map.56 = s16[64,16,128]{2,1,0:T(8,128)(2,1)S(1)} custom-call(s32[2]{0:T(128)S(1)} %copy-done.1, f32[1]{0:T(128)S(6)} %copy.6.ext_ref, s32[1,8]{1,0:T(1,128)S(1)} %copy-done.2, bf16[16,16,1024]{2,1,0:T(8,128)(2,1)S(1)} %get-tuple-element.9.volume_ref, bf16[32,1024]{1,0:T(8,128)(2,1)S(1)} %collective-permute-done.above_ref, ...), custom_call_target="tpu_custom_call" | custom-call | tf_op jit(solution)/shard_map/pallas_call | solution.py:272
  13.1 24.0 %all_to_all.10.parts_ref = s16[64,16,128]{2,1,0:T(8,128)(2,1)S(1)} all-to-all(s16[64,16,128]{2,1,0:T(8,128)(2,1)S(1)} %shard_map.56), channel_id=1, replica_groups=mesh['depth'=64,'tile'=8] {'depth'}, dimensions={0} | all-to-all | bytes 524288 | tf_op jit(solution)/shard_map/all_to_all | solution.py:281
  37.1 0.9 %shard_map.57 = (f32[16,128]{1,0:T(8,128)S(1)}, f32[16,128]{1,0:T(8,128)S(1)}) custom-call(s32[2]{0:T(128)S(1)} %copy-done.1, s16[64,16,128]{2,1,0:T(8,128)(2,1)S(1)} %all_to_all.10.parts_ref), custom_call_target="tpu_custom_call" | custom-call | tf_op jit(solution)/shard_map/pallas_call | solution.py:282
  37.9 4.0 %collective-permute-start.1 = (f32[16,128]{1,0:T(8,128)S(1)}, f32[16,128]{1,0:T(8,128)S(1)}, u32[]{:S(2)}, u32[]{:S(2)}) collective-permute-start(f32[16,128]{1,0:T(8,128)S(1)} %get-tuple-element.12), channel_id=1, source_target_pairs={{0,1},{1,2},{2,3},{3,4},{4,5},{5,6},{6,7},{8,9},{9,10},{10,11},{11... | collective-permute-start | bytes 24584 | tf_op jit(solution)/shard_map/ppermute | solution.py:283
  41.9 0.8 %collective-permute-done.1.back_ref = f32[16,128]{1,0:T(8,128)S(1)} collective-permute-done((f32[16,128]{1,0:T(8,128)S(1)}, f32[16,128]{1,0:T(8,128)S(1)}, u32[]{:S(2)}, u32[]{:S(2)}) %collective-permute-start.1) | collective-permute-done | bytes 8224 | tf_op jit(solution)/shard_map/ppermute | solution.py:283
  42.7 0.1 shard_map.58
  42.8 18.5 %all_to_all.11.whole_ref = s16[64,16,128]{2,1,0:T(8,128)(2,1)S(1)} all-to-all(s16[64,16,128]{2,1,0:T(8,128)(2,1)S(1)} %shard_map.58), channel_id=1, replica_groups=mesh['depth'=64,'tile'=8] {'depth'}, dimensions={0} | all-to-all | bytes 524288 | tf_op jit(solution)/shard_map/all_to_all | solution.py:285
  61.3 0.0 copy-done.3
  61.3 1.7 %shard_map.59 = f32[4,64,1024]{2,1,0:T(8,128)} custom-call(f32[2,3]{1,0:T(2,128)S(1)} %copy-done.3, s16[64,16,128]{2,1,0:T(8,128)(2,1)S(1)} %all_to_all.11.whole_ref), custom_call_target="tpu_custom_call" | custom-call | tf_op jit(solution)/shard_map/pallas_call | solution.py:287
  (1 shorter events, 0.0 us)
Async XLA Ops:
  0.0 7.0 %copy-start = (bf16[16,64,1024]{2,1,0:T(8,128)(2,1)S(1)}, bf16[16,64,1024]{2,1,0:T(8,128)(2,1)}, u32[]{:S(2)}) copy-start(bf16[16,64,1024]{2,1,0:T(8,128)(2,1)} %volume_ref.1) | copy-start | bytes 6291460
  0.0 7.1 %copy-start.2 = (s32[1,8]{1,0:T(1,128)S(1)}, s32[1,8]{1,0:T(1,128)}, u32[]{:S(2)}) copy-start(s32[1,8]{1,0:T(1,128)} %empty_ref.3) | copy-start | bytes 100
  0.0 7.1 %copy-start.1 = (s32[2]{0:T(128)S(1)}, s32[2]{0:T(128)}, u32[]{:S(2)}) copy-start(s32[2]{0:T(128)} %shear_ref.5) | copy-start | bytes 28
  1.6 10.3 %collective-permute-start = (bf16[32,1024]{1,0:T(8,128)(2,1)S(1)}, bf16[32,1024]{1,0:T(8,128)(2,1)S(1)}, u32[]{:S(2)}, u32[]{:S(2)}) collective-permute-start(bf16[32,1024]{1,0:T(8,128)(2,1)S(1)} %reshape.3), channel_id=1, source_target_pairs={{0,1},{1,2},{2,3},{3,4},{4,5},{5,6},{6,7},{8,9},{9,10},{10,11},{11... | collective-permute-start | bytes 196616 | tf_op jit(solution)/shard_map/ppermute | solution.py:262
  7.1 54.2 %copy-start.3 = (f32[2,3]{1,0:T(2,128)S(1)}, f32[2,3]{1,0:T(2,128)}, u32[]{:S(2)}) copy-start(f32[2,3]{1,0:T(2,128)} %palette_ref.1) | copy-start | bytes 76
  37.9 4.8 %collective-permute-start.1 = (f32[16,128]{1,0:T(8,128)S(1)}, f32[16,128]{1,0:T(8,128)S(1)}, u32[]{:S(2)}, u32[]{:S(2)}) collective-permute-start(f32[16,128]{1,0:T(8,128)S(1)} %get-tuple-element.12), channel_id=1, source_target_pairs={{0,1},{1,2},{2,3},{3,4},{4,5},{5,6},{6,7},{8,9},{9,10},{10,11},{11... | collective-permute-start | bytes 24584 | tf_op jit(solution)/shard_map/ppermute | solution.py:283

commit v4 on v3

--- a/solution.py
+++ b/solution.py
@@ -136,7 +136,7 @@
     own_count = empty_ref[0, tile_pos]
     col_base = (shear_ref[0] * depth_idx) >> 1
 
-    @pl.loop(0, SLAB)
+    @pl.loop(0, SLAB, unroll=SLAB)
     def _(i):
         rel, near, far = column_terms(shear_ref, depth_idx * SLAB + i, col_base)
         live = (i >= own_count).astype(jnp.float32)
@@ -146,13 +146,13 @@
             for j in range(BLOCKS):
                 lines[i, j, HALO + c * 16 : HALO + (c + 1) * 16, :] = blocks[j]
 
-    @pl.loop(1, ROWS // 8)
+    @pl.loop(1, ROWS // 8, unroll=ROWS // 8 - 1)
     def _(c):
         march_rows(c * 8, depth_idx, shear_ref, sigma, lines, stage, c * 8)
 
     row_base = (shear_ref[1] * depth_idx) >> 3
 
-    @pl.loop(8, ROWS, step=8)
+    @pl.loop(8, ROWS, step=8, unroll=ROWS // 8 - 1)
     def _(first):
         for r in range(8):
             piece = stage[pl.ds((first + r) * 16, 16), :]
@@ -187,20 +187,26 @@
 
 
 def compose_kernel(shear_ref, parts_ref, front_ref, back_ref):
-    row = lax.axis_index("depth")
+    limit = jnp.full((8, LANES), 8 * lax.axis_index("depth") + 8, jnp.int32)
+    slope = jnp.full((8, LANES), shear_ref[1], jnp.int32)
     zero = jnp.zeros((8, LANES), jnp.float32)
-    totals = [zero, zero]
-    lights = [zero, zero]
+    reach = jnp.zeros((8, LANES), jnp.int32)
+    total, front_total, front_light, back_light = zero, zero, zero, zero
     for d in range(DEPTH):
         codes = parts_ref[d].astype(jnp.int32)
         depth = depth_from_code(codes[:8], BRICK_RANGE)
-        light = from_code(codes[8:]) * (math.log(2.0) / TOP) * depth
-        is_back = (((shear_ref[1] * d) >> 3) > row).astype(jnp.float32)
-        for side, use in enumerate((1.0 - is_back, is_back)):
-            lights[side] = lights[side] + (use * jnp.exp2(-totals[side])) * light
-            totals[side] = totals[side] + use * depth
-    front_ref[0:8, :], front_ref[8:16, :] = totals[0], lights[0]
-    back_ref[0:8, :], back_ref[8:16, :] = totals[1], lights[1]
+        light = from_code(codes[8:]) * depth * jnp.exp2(-total)
+        in_front = reach < limit
+        front_total = jnp.where(in_front, front_total + depth, front_total)
+        front_light = jnp.where(in_front, front_light + light, front_light)
+        back_light = jnp.where(in_front, back_light, back_light + light)
+        total = total + depth
+        reach = reach + slope
+    scale = math.log(2.0) / TOP
+    front_ref[0:8, :] = front_total
+    front_ref[8:16, :] = front_light * scale
+    back_ref[0:8, :] = total - front_total
+    back_ref[8:16, :] = back_light * scale * jnp.exp2(front_total)
 
 
 def spread_kernel(front_ref, back_ref, out_ref):

time: 63.6 us -> 62.3 us (0.980)
  Pallas kernels: 8.5 us -> 7.26 us
    pallas_call x1, Pallas kernels: 4.73 us -> 3.55 us  [per_device(): call(bulk_kernel, parts_shape, [SMEM, SMEM, SMEM, VMEM], [pltpu.VMEM((SLA...]
  transfers between devices with their start and end apart: 2 -> 2, of which waited for: 1 -> 1; matrix products, arithmetic and copies ran while one was open for 0% -> 0% of each run, Pallas kernels for 8% -> 6%
where the time goes in v4:
time: 62.3 us; the launch traced here: 61.7 us
  blocking collectives  42.5 us (68%)
  starting transfers between devices  8.83 us (14%)
  Pallas kernels  7.26 us (12%)
  local copies, waits for them, and re-layouts  1.55 us (2%)
  waiting for transfers between devices  0.78 us (1%)
  between operations  0.75 us (1%)
    all_to_all x1, blocking collectives, per_device(): parts = lax.all_to_all(parts, 'depth', 0, 0, tiled=True)  24 us
    all_to_all x1, blocking collectives, per_device(): whole = lax.all_to_all(copies, 'depth', 0, 0, tiled=True)  18.5 us
    ppermute x1, starting transfers between devices, per_device(): above = lax.ppermute(last[:, 14:, :].reshape(2 * SLAB, WIDTH), 'tile', down)  4.83 us
    ppermute x1, starting transfers between devices, per_device(): back = lax.ppermute(back, 'tile', down)  4 us
    pallas_call x1, Pallas kernels, per_device(): call(bulk_kernel, parts_shape, [SMEM, SMEM, SMEM, VMEM], [pltpu.VMEM((SLA...  3.55 us
    pallas_call x1, Pallas kernels, per_device(): call(image_kernel, image_shape, [SMEM, VMEM], [pltpu.VMEM((ROWS * 16, LAN...  1.65 us
    slice x1, local copies, waits for them, and re-layouts, per_device(): volume[:, ROWS - 16:, :]  1.43 us
  transfers between devices with their start and end apart: 2, of which 1 were waited for; matrix products, arithmetic and copies ran while one was open for 0% of the time, Pallas kernels for 6%

profile of v4, /device:TPU:1, one launch (start us, length us, event | category | flops | bytes accessed | tf_op | source)
XLA Modules:
  0.0 61.7 jit_solution(4175731784664319712)
XLA Ops:
  0.0 0.0 copy-start
  0.0 0.0 copy-start.2
  0.0 0.0 copy-start.1
  0.0 1.4 %fusion = (bf16[16,16,1024]{2,1,0:T(8,128)(2,1)S(1)}, bf16[16,16,1024]{2,1,0:T(8,128)(2,1)S(1)}) fusion(bf16[16,64,1024]{2,1,0:T(8,128)(2,1)} %volume_ref.1), kind=kLoop, calls=%fused_computation | loop fusion | bytes 2097152 | tf_op jit(solution)/shard_map/slice | solution.py:267
  1.4 0.1 slice.11
  1.6 4.8 %collective-permute-start = (bf16[32,1024]{1,0:T(8,128)(2,1)S(1)}, bf16[32,1024]{1,0:T(8,128)(2,1)S(1)}, u32[]{:S(2)}, u32[]{:S(2)}) collective-permute-start(bf16[32,1024]{1,0:T(8,128)(2,1)S(1)} %reshape.3), channel_id=1, source_target_pairs={{0,1},{1,2},{2,3},{3,4},{4,5},{5,6},{6,7},{8,9},{9,10},{10,11},{11... | collective-permute-start | bytes 196616 | tf_op jit(solution)/shard_map/ppermute | solution.py:268
  7.0 0.0 copy-done
  7.1 0.0 copy-done.2
  7.1 0.0 copy-done.1
  7.1 0.0 copy-start.3
  7.1 3.6 %shard_map.55.bulk_ref = s16[64,16,128]{2,1,0:T(8,128)(2,1)S(1)} custom-call(s32[2]{0:T(128)S(1)} %copy-done.1, f32[1]{0:T(128)S(6)} %copy.6.ext_ref, s32[1,8]{1,0:T(1,128)S(1)} %copy-done.2, bf16[16,64,1024]{2,1,0:T(8,128)(2,1)S(1)} %copy-done), custom_call_target="tpu_custom_call" | custom-call | tf_op jit(solution)/shard_map/pallas_call | solution.py:269
  10.6 0.0 collective-permute-done.above_ref
  10.7 1.2 %shard_map.56 = s16[64,16,128]{2,1,0:T(8,128)(2,1)S(1)} custom-call(s32[2]{0:T(128)S(1)} %copy-done.1, f32[1]{0:T(128)S(6)} %copy.6.ext_ref, s32[1,8]{1,0:T(1,128)S(1)} %copy-done.2, bf16[16,16,1024]{2,1,0:T(8,128)(2,1)S(1)} %get-tuple-element.9.volume_ref, bf16[32,1024]{1,0:T(8,128)(2,1)S(1)} %collective-permute-done.above_ref, ...), custom_call_target="tpu_custom_call" | custom-call | tf_op jit(solution)/shard_map/pallas_call | solution.py:278
  11.9 24.0 %all_to_all.10.parts_ref = s16[64,16,128]{2,1,0:T(8,128)(2,1)S(1)} all-to-all(s16[64,16,128]{2,1,0:T(8,128)(2,1)S(1)} %shard_map.56), channel_id=1, replica_groups=mesh['depth'=64,'tile'=8] {'depth'}, dimensions={0} | all-to-all | bytes 524288 | tf_op jit(solution)/shard_map/all_to_all | solution.py:287
  35.9 0.8 %shard_map.57 = (f32[16,128]{1,0:T(8,128)S(1)}, f32[16,128]{1,0:T(8,128)S(1)}) custom-call(s32[2]{0:T(128)S(1)} %copy-done.1, s16[64,16,128]{2,1,0:T(8,128)(2,1)S(1)} %all_to_all.10.parts_ref), custom_call_target="tpu_custom_call" | custom-call | tf_op jit(solution)/shard_map/pallas_call | solution.py:288
  36.7 4.0 %collective-permute-start.1 = (f32[16,128]{1,0:T(8,128)S(1)}, f32[16,128]{1,0:T(8,128)S(1)}, u32[]{:S(2)}, u32[]{:S(2)}) collective-permute-start(f32[16,128]{1,0:T(8,128)S(1)} %get-tuple-element.12), channel_id=1, source_target_pairs={{0,1},{1,2},{2,3},{3,4},{4,5},{5,6},{6,7},{8,9},{9,10},{10,11},{11... | collective-permute-start | bytes 24584 | tf_op jit(solution)/shard_map/ppermute | solution.py:289
  40.7 0.8 %collective-permute-done.1.back_ref = f32[16,128]{1,0:T(8,128)S(1)} collective-permute-done((f32[16,128]{1,0:T(8,128)S(1)}, f32[16,128]{1,0:T(8,128)S(1)}, u32[]{:S(2)}, u32[]{:S(2)}) %collective-permute-start.1) | collective-permute-done | bytes 8224 | tf_op jit(solution)/shard_map/ppermute | solution.py:289
  41.5 0.1 shard_map.58
  41.5 18.5 %all_to_all.11.whole_ref = s16[64,16,128]{2,1,0:T(8,128)(2,1)S(1)} all-to-all(s16[64,16,128]{2,1,0:T(8,128)(2,1)S(1)} %shard_map.58), channel_id=1, replica_groups=mesh['depth'=64,'tile'=8] {'depth'}, dimensions={0} | all-to-all | bytes 524288 | tf_op jit(solution)/shard_map/all_to_all | solution.py:291
  60.0 0.0 copy-done.3
  60.0 1.7 %shard_map.59 = f32[4,64,1024]{2,1,0:T(8,128)} custom-call(f32[2,3]{1,0:T(2,128)S(1)} %copy-done.3, s16[64,16,128]{2,1,0:T(8,128)(2,1)S(1)} %all_to_all.11.whole_ref), custom_call_target="tpu_custom_call" | custom-call | tf_op jit(solution)/shard_map/pallas_call | solution.py:293
  (1 shorter events, 0.0 us)
Async XLA Ops:
  0.0 7.0 %copy-start = (bf16[16,64,1024]{2,1,0:T(8,128)(2,1)S(1)}, bf16[16,64,1024]{2,1,0:T(8,128)(2,1)}, u32[]{:S(2)}) copy-start(bf16[16,64,1024]{2,1,0:T(8,128)(2,1)} %volume_ref.1) | copy-start | bytes 6291460
  0.0 7.1 %copy-start.2 = (s32[1,8]{1,0:T(1,128)S(1)}, s32[1,8]{1,0:T(1,128)}, u32[]{:S(2)}) copy-start(s32[1,8]{1,0:T(1,128)} %empty_ref.3) | copy-start | bytes 100
  0.0 7.1 %copy-start.1 = (s32[2]{0:T(128)S(1)}, s32[2]{0:T(128)}, u32[]{:S(2)}) copy-start(s32[2]{0:T(128)} %shear_ref.5) | copy-start | bytes 28
  1.6 9.1 %collective-permute-start = (bf16[32,1024]{1,0:T(8,128)(2,1)S(1)}, bf16[32,1024]{1,0:T(8,128)(2,1)S(1)}, u32[]{:S(2)}, u32[]{:S(2)}) collective-permute-start(bf16[32,1024]{1,0:T(8,128)(2,1)S(1)} %reshape.3), channel_id=1, source_target_pairs={{0,1},{1,2},{2,3},{3,4},{4,5},{5,6},{6,7},{8,9},{9,10},{10,11},{11... | collective-permute-start | bytes 196616 | tf_op jit(solution)/shard_map/ppermute | solution.py:268
  7.1 53.0 %copy-start.3 = (f32[2,3]{1,0:T(2,128)S(1)}, f32[2,3]{1,0:T(2,128)}, u32[]{:S(2)}) copy-start(f32[2,3]{1,0:T(2,128)} %palette_ref.1) | copy-start | bytes 76
  36.7 4.8 %collective-permute-start.1 = (f32[16,128]{1,0:T(8,128)S(1)}, f32[16,128]{1,0:T(8,128)S(1)}, u32[]{:S(2)}, u32[]{:S(2)}) collective-permute-start(f32[16,128]{1,0:T(8,128)S(1)} %get-tuple-element.12), channel_id=1, source_target_pairs={{0,1},{1,2},{2,3},{3,4},{4,5},{5,6},{6,7},{8,9},{9,10},{10,11},{11... | collective-permute-start | bytes 24584 | tf_op jit(solution)/shard_map/ppermute | solution.py:289

commit v5 on v4

--- a/solution.py
+++ b/solution.py
@@ -104,7 +104,7 @@
     return (num >> 7) - base, 1.0 - far, far
 
 
-def march_rows(first, depth_idx, shear_ref, sigma, lines, stage, stage_row):
+def march_rows(first, depth_idx, shear_ref, sigma, lines, turned):
     row_base = (shear_ref[1] * depth_idx) >> 3
     total = [jnp.zeros((8, LANES), jnp.float32) for _ in range(BLOCKS)]
     light = [jnp.zeros((8, LANES), jnp.float32) for _ in range(BLOCKS)]
@@ -125,11 +125,11 @@
     total = shift_columns(total, col_base)
     light = shift_columns([scale * value for value in light], col_base)
     for j in range(BLOCKS):
-        stage[pl.ds(stage_row * 16 + j, 8, stride=16), :] = total[j]
-        stage[pl.ds(stage_row * 16 + 8 + j, 8, stride=16), :] = light[j]
-
-
-def bulk_kernel(shear_ref, ext_ref, empty_ref, volume_ref, out_ref, lines, stage):
+        turned[0, j, pl.ds(row_base + first, 8), :] = total[j]
+        turned[1, j, pl.ds(row_base + first, 8), :] = light[j]
+
+
+def bulk_kernel(shear_ref, ext_ref, empty_ref, first_ref, volume_ref, turned_ref, top_ref, lines):
     depth_idx = lax.axis_index("depth")
     tile_pos = lax.axis_index("tile")
     sigma = ext_ref[0] * (4.0 / 1024.0 * math.log2(math.e))
@@ -141,53 +141,58 @@
         rel, near, far = column_terms(shear_ref, depth_idx * SLAB + i, col_base)
         live = (i >= own_count).astype(jnp.float32)
         for c in range(ROWS // 16):
-            plane = volume_ref[i, c * 16 : (c + 1) * 16, :].astype(jnp.float32)
+            plane = volume_ref[i, c * 16 : (c + 1) * 16, :] if c else first_ref[i]
+            plane = plane.astype(jnp.float32)
             blocks = column_lerp(plane, rel, near * live, far * live)
             for j in range(BLOCKS):
                 lines[i, j, HALO + c * 16 : HALO + (c + 1) * 16, :] = blocks[j]
+                if c == 0:
+                    top_ref[i, j] = blocks[j][:8]
 
     @pl.loop(1, ROWS // 8, unroll=ROWS // 8 - 1)
     def _(c):
-        march_rows(c * 8, depth_idx, shear_ref, sigma, lines, stage, c * 8)
-
-    row_base = (shear_ref[1] * depth_idx) >> 3
-
-    @pl.loop(8, ROWS, step=8, unroll=ROWS // 8 - 1)
-    def _(first):
-        for r in range(8):
-            piece = stage[pl.ds((first + r) * 16, 16), :]
-            out_ref[(row_base + first + r) & (ROWS - 1)] = encode_brick(piece[:8], piece[8:])
-
-
-def edge_kernel(shear_ref, ext_ref, empty_ref, volume_ref, above_ref, bulk_ref, out_ref, lines, stage):
+        march_rows(c * 8, depth_idx, shear_ref, sigma, lines, turned_ref)
+
+
+def edge_kernel(
+    shear_ref, ext_ref, empty_ref, top_ref, above_ref, turned_ref, out_ref, lines, edge
+):
     depth_idx = lax.axis_index("depth")
     tile_pos = lax.axis_index("tile")
     sigma = ext_ref[0] * (4.0 / 1024.0 * math.log2(math.e))
-    own_count = empty_ref[0, tile_pos]
     above_count = empty_ref[0, jnp.maximum(tile_pos - 1, 0)]
     col_base = (shear_ref[0] * depth_idx) >> 1
     row_base = (shear_ref[1] * depth_idx) >> 3
-    out_ref[...] = bulk_ref[...]
     above = above_ref[...].astype(jnp.float32)
     for i in range(SLAB):
         rel, near, far = column_terms(shear_ref, depth_idx * SLAB + i, col_base)
-        live = (i >= own_count).astype(jnp.float32)
-        plane = volume_ref[i].astype(jnp.float32)[:8]
-        blocks = column_lerp(plane, rel, near * live, far * live)
         live = (i >= above_count).astype(jnp.float32)
         halos = column_lerp(above[2 * i : 2 * i + 2], rel, near * live, far * live)
         for j in range(BLOCKS):
-            lines[i, j, HALO : HALO + 8, :] = blocks[j]
+            lines[i, j, HALO : HALO + 8, :] = top_ref[i, j]
             lines[i, j, HALO - 2 : HALO, :] = halos[j]
 
-    march_rows(0, depth_idx, shear_ref, sigma, lines, stage, 0)
-    for r in range(8):
-        piece = stage[r * 16 : (r + 1) * 16, :]
-        out_ref[(row_base + r) & (ROWS - 1)] = encode_brick(piece[:8], piece[8:])
+    march_rows(0, depth_idx, shear_ref, sigma, lines, edge)
+    for g in range(ROWS // 8):
+        row = lax.broadcasted_iota(jnp.int32, (8, LANES), 0) + 8 * g
+        next_tile = row < row_base
+        at_edge = row < row_base + 8
+        rows = slice(8 * g, 8 * g + 8)
+        for j in range(BLOCKS):
+            total, light = [
+                jnp.where(
+                    next_tile,
+                    turned_ref[k, j, ROWS + 8 * g : ROWS + 8 * g + 8, :],
+                    jnp.where(at_edge, edge[k, j, rows, :], turned_ref[k, j, rows, :]),
+                )
+                for k in range(2)
+            ]
+            out_ref[g * BLOCKS + j] = encode_brick(total, light)
 
 
 def compose_kernel(shear_ref, parts_ref, front_ref, back_ref):
-    limit = jnp.full((8, LANES), 8 * lax.axis_index("depth") + 8, jnp.int32)
+    row = lax.broadcasted_iota(jnp.int32, (8, LANES), 0) + (lax.axis_index("depth") >> 3) * 8
+    limit = 8 * row + 8
     slope = jnp.full((8, LANES), shear_ref[1], jnp.int32)
     zero = jnp.zeros((8, LANES), jnp.float32)
     reach = jnp.zeros((8, LANES), jnp.int32)
@@ -220,30 +225,23 @@
         out_ref[p] = codes
 
 
-def image_kernel(palette_ref, whole_ref, image_hbm, stage, image, sems):
+def image_kernel(palette_ref, whole_ref, image_hbm, image, sems):
     base = [palette_ref[0, k] for k in range(3)]
     slope = [palette_ref[1, k] for k in range(3)]
     copies = []
-    for c in range(ROWS // 8):
-        rows = slice(c * 8, (c + 1) * 8)
-        for r in range(c * 8, c * 8 + 8):
-            codes = whole_ref[r].astype(jnp.int32)
-            opacity = 1.0 - jnp.exp2(-depth_from_code(codes[:8], IMAGE_RANGE))
-            stage[r * 16 : r * 16 + 8, :] = opacity
-            stage[r * 16 + 8 : r * 16 + 16, :] = from_code(codes[8:]) * (1.0 / TOP) * opacity
+    for g in range(ROWS // 8):
+        rows = slice(g * 8, (g + 1) * 8)
         for j in range(BLOCKS):
             columns = slice(j * LANES, (j + 1) * LANES)
-            opacity = stage[pl.ds(c * 128 + j, 8, stride=16), :]
-            light = stage[pl.ds(c * 128 + 8 + j, 8, stride=16), :]
+            codes = whole_ref[g * BLOCKS + j].astype(jnp.int32)
+            opacity = 1.0 - jnp.exp2(-depth_from_code(codes[:8], IMAGE_RANGE))
+            light = from_code(codes[8:]) * (1.0 / TOP) * opacity
             for k in range(3):
                 image[k, rows, columns] = base[k] * opacity + slope[k] * light
             image[3, rows, columns] = opacity
-        if c % 2:
-            part = pl.ds(c * 8 - 8, 16)
-            copies.append(
-                pltpu.make_async_copy(image.at[:, part], image_hbm.at[:, part], sems.at[c // 2])
-            )
-            copies[-1].start()
+        part = pl.ds(g * 8, 8)
+        copies.append(pltpu.make_async_copy(image.at[:, part], image_hbm.at[:, part], sems.at[g]))
+        copies[-1].start()
     for copy in copies:
         copy.wait()
 
@@ -266,24 +264,24 @@
     down = [(i, i + 1) for i in range(TILES - 1)]
     first, last = lax.optimization_barrier((volume[:, :16, :], volume[:, ROWS - 16 :, :]))
     above = lax.ppermute(last[:, 14:, :].reshape(2 * SLAB, WIDTH), "tile", down)
-    bulk = call(
+    turned, top = call(
         bulk_kernel,
-        parts_shape,
-        [SMEM, SMEM, SMEM, VMEM],
-        [
-            pltpu.VMEM((SLAB, BLOCKS, HALO + ROWS, LANES), f32),
-            pltpu.VMEM((ROWS * 16, LANES), f32),
-        ],
-    )(shear, extinction, empty_slices, volume)
+        (
+            jax.ShapeDtypeStruct((2, BLOCKS, 2 * ROWS, LANES), f32),
+            jax.ShapeDtypeStruct((SLAB, BLOCKS, 8, LANES), f32),
+        ),
+        [SMEM, SMEM, SMEM, VMEM, VMEM],
+        [pltpu.VMEM((SLAB, BLOCKS, HALO + ROWS, LANES), f32)],
+    )(shear, extinction, empty_slices, first, volume)
     parts = call(
         edge_kernel,
         parts_shape,
         [SMEM, SMEM, SMEM, VMEM, VMEM, VMEM],
         [
             pltpu.VMEM((SLAB, BLOCKS, HALO + 8, LANES), f32),
-            pltpu.VMEM((8 * 16, LANES), f32),
+            pltpu.VMEM((2, BLOCKS, ROWS, LANES), f32),
         ],
-    )(shear, extinction, empty_slices, first, above, bulk)
+    )(shear, extinction, empty_slices, top, above, turned)
     parts = lax.all_to_all(parts, "depth", 0, 0, tiled=True)
     front, back = call(compose_kernel, (piece_shape, piece_shape), [SMEM, VMEM])(shear, parts)
     back = lax.ppermute(back, "tile", down)
@@ -295,9 +293,8 @@
         image_shape,
         [SMEM, VMEM],
         [
-            pltpu.VMEM((ROWS * 16, LANES), f32),
             pltpu.VMEM((4, ROWS, WIDTH), f32),
-            pltpu.SemaphoreType.DMA((ROWS // 16,)),
+            pltpu.SemaphoreType.DMA((ROWS // 8,)),
         ],
         pl.BlockSpec(memory_space=pl.ANY),
     )(palette, whole)

time: 62.3 us -> 62 us (level)
  transfers between devices with their start and end apart: 2 -> 2, of which waited for: 1 -> 1; matrix products, arithmetic and copies ran while one was open for 0% -> 0% of each run, Pallas kernels for 6% -> 5%
where the time goes in v5:
time: 62 us; the launch traced here: 61.4 us
  blocking collectives  42.6 us (69%)
  starting transfers between devices  8.82 us (14%)
  Pallas kernels  6.94 us (11%)
  local copies, waits for them, and re-layouts  1.54 us (2%)
  waiting for transfers between devices  0.78 us (1%)
  between operations  0.75 us (1%)
    all_to_all x1, blocking collectives, per_device(): parts = lax.all_to_all(parts, 'depth', 0, 0, tiled=True)  24 us
    all_to_all x1, blocking collectives, per_device(): whole = lax.all_to_all(copies, 'depth', 0, 0, tiled=True)  18.5 us
    ppermute x1, starting transfers between devices, per_device(): above = lax.ppermute(last[:, 14:, :].reshape(2 * SLAB, WIDTH), 'tile', down)  4.83 us
    ppermute x1, starting transfers between devices, per_device(): back = lax.ppermute(back, 'tile', down)  4 us
    pallas_call x1, Pallas kernels, per_device(): call(bulk_kernel, (jax.ShapeDtypeStruct((2, BLOCKS, 2 * ROWS, LANES), f32...  3.18 us
    pallas_call x1, Pallas kernels, per_device(): call(image_kernel, image_shape, [SMEM, VMEM], [pltpu.VMEM((4, ROWS, WIDTH...  1.61 us
    slice x1, local copies, waits for them, and re-layouts, per_device(): volume[:, ROWS - 16:, :]  1.43 us
    pallas_call x1, Pallas kernels, per_device(): call(edge_kernel, parts_shape, [SMEM, SMEM, SMEM, VMEM, VMEM, VMEM], [plt...  1.3 us
  transfers between devices with their start and end apart: 2, of which 1 were waited for; matrix products, arithmetic and copies ran while one was open for 0% of the time, Pallas kernels for 5%

profile of v5, /device:TPU:1, one launch (start us, length us, event | category | flops | bytes accessed | tf_op | source)
XLA Modules:
  0.0 61.4 jit_solution(6003637231914409325)
XLA Ops:
  0.0 0.0 copy-start
  0.0 0.0 copy-start.1
  0.0 0.0 copy-start.2
  0.0 1.4 %fusion = (bf16[16,16,1024]{2,1,0:T(8,128)(2,1)S(1)}, bf16[16,16,1024]{2,1,0:T(8,128)(2,1)S(1)}) fusion(bf16[16,64,1024]{2,1,0:T(8,128)(2,1)} %volume_ref.1), kind=kLoop, calls=%fused_computation | loop fusion | bytes 2097152 | tf_op jit(solution)/shard_map/slice | solution.py:265
  1.4 0.1 slice.11
  1.6 4.8 %collective-permute-start = (bf16[32,1024]{1,0:T(8,128)(2,1)S(1)}, bf16[32,1024]{1,0:T(8,128)(2,1)S(1)}, u32[]{:S(2)}, u32[]{:S(2)}) collective-permute-start(bf16[32,1024]{1,0:T(8,128)(2,1)S(1)} %reshape.3), channel_id=1, source_target_pairs={{0,1},{1,2},{2,3},{3,4},{4,5},{5,6},{6,7},{8,9},{9,10},{10,11},{11... | collective-permute-start | bytes 196616 | tf_op jit(solution)/shard_map/ppermute | solution.py:266
  7.0 0.0 copy-done
  7.1 0.0 copy-done.1
  7.1 0.0 copy-done.2
  7.1 3.2 %shard_map.55 = (f32[2,8,128,128]{3,2,1,0:T(8,128)S(1)}, f32[16,8,8,128]{3,2,1,0:T(8,128)S(1)}) custom-call(s32[2]{0:T(128)S(1)} %copy-done.1, f32[1]{0:T(128)S(6)} %copy.6.ext_ref, s32[1,8]{1,0:T(1,128)S(1)} %copy-done.2, bf16[16,16,1024]{2,1,0:T(8,128)(2,1)S(1)} %get-tuple-element.11.first_ref, bf16[16,64,1024]{2,1,0:T(8,128)(2,1)S(1)} %copy-done), custom_call_target="tpu_custom_call" | custom-call | tf_op jit(solution)/shard_map/pallas_call | solution.py:267
  10.3 0.0 copy-start.3
  10.3 0.0 collective-permute-done.above_ref
  10.3 1.3 %shard_map.56 = s16[64,16,128]{2,1,0:T(8,128)(2,1)S(1)} custom-call(s32[2]{0:T(128)S(1)} %copy-done.1, f32[1]{0:T(128)S(6)} %copy.6.ext_ref, s32[1,8]{1,0:T(1,128)S(1)} %copy-done.2, f32[16,8,8,128]{3,2,1,0:T(8,128)S(1)} %get-tuple-element.12.top_ref, bf16[32,1024]{1,0:T(8,128)(2,1)S(1)} %collective-permute-done.above_ref, ...), custom_call_target="tpu_custom_call" | custom-call | tf_op jit(solution)/shard_map/pallas_call | solution.py:276
  11.6 24.0 %all_to_all.10.parts_ref = s16[64,16,128]{2,1,0:T(8,128)(2,1)S(1)} all-to-all(s16[64,16,128]{2,1,0:T(8,128)(2,1)S(1)} %shard_map.56), channel_id=1, replica_groups=mesh['depth'=64,'tile'=8] {'depth'}, dimensions={0} | all-to-all | bytes 524288 | tf_op jit(solution)/shard_map/all_to_all | solution.py:285
  35.6 0.8 %shard_map.57 = (f32[16,128]{1,0:T(8,128)S(1)}, f32[16,128]{1,0:T(8,128)S(1)}) custom-call(s32[2]{0:T(128)S(1)} %copy-done.1, s16[64,16,128]{2,1,0:T(8,128)(2,1)S(1)} %all_to_all.10.parts_ref), custom_call_target="tpu_custom_call" | custom-call | tf_op jit(solution)/shard_map/pallas_call | solution.py:286
  36.4 4.0 %collective-permute-start.1 = (f32[16,128]{1,0:T(8,128)S(1)}, f32[16,128]{1,0:T(8,128)S(1)}, u32[]{:S(2)}, u32[]{:S(2)}) collective-permute-start(f32[16,128]{1,0:T(8,128)S(1)} %get-tuple-element.16), channel_id=1, source_target_pairs={{0,1},{1,2},{2,3},{3,4},{4,5},{5,6},{6,7},{8,9},{9,10},{10,11},{11... | collective-permute-start | bytes 24584 | tf_op jit(solution)/shard_map/ppermute | solution.py:287
  40.4 0.8 %collective-permute-done.1.back_ref = f32[16,128]{1,0:T(8,128)S(1)} collective-permute-done((f32[16,128]{1,0:T(8,128)S(1)}, f32[16,128]{1,0:T(8,128)S(1)}, u32[]{:S(2)}, u32[]{:S(2)}) %collective-permute-start.1) | collective-permute-done | bytes 8224 | tf_op jit(solution)/shard_map/ppermute | solution.py:287
  41.2 0.1 shard_map.58
  41.3 18.5 %all_to_all.11.whole_ref = s16[64,16,128]{2,1,0:T(8,128)(2,1)S(1)} all-to-all(s16[64,16,128]{2,1,0:T(8,128)(2,1)S(1)} %shard_map.58), channel_id=1, replica_groups=mesh['depth'=64,'tile'=8] {'depth'}, dimensions={0} | all-to-all | bytes 524288 | tf_op jit(solution)/shard_map/all_to_all | solution.py:289
  59.8 0.0 copy-done.3
  59.8 1.6 %shard_map.59 = f32[4,64,1024]{2,1,0:T(8,128)} custom-call(f32[2,3]{1,0:T(2,128)S(1)} %copy-done.3, s16[64,16,128]{2,1,0:T(8,128)(2,1)S(1)} %all_to_all.11.whole_ref), custom_call_target="tpu_custom_call" | custom-call | tf_op jit(solution)/shard_map/pallas_call | solution.py:291
  (1 shorter events, 0.0 us)
Async XLA Ops:
  0.0 7.0 %copy-start = (bf16[16,64,1024]{2,1,0:T(8,128)(2,1)S(1)}, bf16[16,64,1024]{2,1,0:T(8,128)(2,1)}, u32[]{:S(2)}) copy-start(bf16[16,64,1024]{2,1,0:T(8,128)(2,1)} %volume_ref.1) | copy-start | bytes 6291460
  0.0 7.1 %copy-start.1 = (s32[2]{0:T(128)S(1)}, s32[2]{0:T(128)}, u32[]{:S(2)}) copy-start(s32[2]{0:T(128)} %shear_ref.5) | copy-start | bytes 28
  0.0 7.1 %copy-start.2 = (s32[1,8]{1,0:T(1,128)S(1)}, s32[1,8]{1,0:T(1,128)}, u32[]{:S(2)}) copy-start(s32[1,8]{1,0:T(1,128)} %empty_ref.3) | copy-start | bytes 100
  1.6 8.7 %collective-permute-start = (bf16[32,1024]{1,0:T(8,128)(2,1)S(1)}, bf16[32,1024]{1,0:T(8,128)(2,1)S(1)}, u32[]{:S(2)}, u32[]{:S(2)}) collective-permute-start(bf16[32,1024]{1,0:T(8,128)(2,1)S(1)} %reshape.3), channel_id=1, source_target_pairs={{0,1},{1,2},{2,3},{3,4},{4,5},{5,6},{6,7},{8,9},{9,10},{10,11},{11... | collective-permute-start | bytes 196616 | tf_op jit(solution)/shard_map/ppermute | solution.py:266
  10.3 49.5 %copy-start.3 = (f32[2,3]{1,0:T(2,128)S(1)}, f32[2,3]{1,0:T(2,128)}, u32[]{:S(2)}) copy-start(f32[2,3]{1,0:T(2,128)} %palette_ref.1) | copy-start | bytes 76
  36.4 4.8 %collective-permute-start.1 = (f32[16,128]{1,0:T(8,128)S(1)}, f32[16,128]{1,0:T(8,128)S(1)}, u32[]{:S(2)}, u32[]{:S(2)}) collective-permute-start(f32[16,128]{1,0:T(8,128)S(1)} %get-tuple-element.16), channel_id=1, source_target_pairs={{0,1},{1,2},{2,3},{3,4},{4,5},{5,6},{6,7},{8,9},{9,10},{10,11},{11... | collective-permute-start | bytes 24584 | tf_op jit(solution)/shard_map/ppermute | solution.py:287

commit v6 on v5

--- a/solution.py
+++ b/solution.py
@@ -26,12 +26,16 @@
 
 
 def to_code(value):
-    whole = (jnp.clip(value, 0.0, TOP) + 0.5).astype(jnp.int32)
-    return whole - 32768
-
-
-def from_code(code):
-    return (code.astype(jnp.int32) + 32768).astype(jnp.float32)
+    return (jnp.clip(value, 0.0, TOP) + 0.5).astype(jnp.int32)
+
+
+def pair(above, below):
+    return lax.shift_left(above, 16) | below
+
+
+def unpair(codes):
+    above = lax.shift_right_logical(codes, 16)
+    return above.astype(jnp.float32), (codes & 0xFFFF).astype(jnp.float32)
 
 
 def depth_to_code(depth, limits):
@@ -42,9 +46,8 @@
     return to_code(jnp.where(seen, level, 0.0))
 
 
-def depth_from_code(code, limits):
+def depth_from_level(level, limits):
     low, high = limits
-    level = from_code(code)
     depth = jnp.exp2((level - 1.0) * ((high - low) / (TOP - 1.0)) + low)
     return jnp.where(level > 0.5, depth, 0.0)
 
@@ -53,8 +56,7 @@
     depth = -total
     seen = depth >= 2.0 ** BRICK_RANGE[0]
     mean = light / (jnp.where(seen, depth, 1.0) * math.log(2.0))
-    codes = [depth_to_code(depth, BRICK_RANGE), to_code(jnp.where(seen, mean * TOP, 0.0))]
-    return jnp.concatenate(codes, axis=0).astype(jnp.int16)
+    return pair(depth_to_code(depth, BRICK_RANGE), to_code(jnp.where(seen, mean * TOP, 0.0)))
 
 
 def lane_index(rows):
@@ -129,12 +131,14 @@
         turned[1, j, pl.ds(row_base + first, 8), :] = light[j]
 
 
-def bulk_kernel(shear_ref, ext_ref, empty_ref, first_ref, volume_ref, turned_ref, top_ref, lines):
+def bulk_kernel(shear_ref, ext_ref, empty_ref, first_ref, volume_ref, turned_ref, top_ref, slope_ref, lines):
     depth_idx = lax.axis_index("depth")
     tile_pos = lax.axis_index("tile")
     sigma = ext_ref[0] * (4.0 / 1024.0 * math.log2(math.e))
     own_count = empty_ref[0, tile_pos]
     col_base = (shear_ref[0] * depth_idx) >> 1
+
+    slope_ref[...] = jnp.full((8, LANES), shear_ref[1], jnp.int32)
 
     @pl.loop(0, SLAB, unroll=SLAB)
     def _(i):
@@ -190,17 +194,17 @@
             out_ref[g * BLOCKS + j] = encode_brick(total, light)
 
 
-def compose_kernel(shear_ref, parts_ref, front_ref, back_ref):
+def compose_kernel(slope_ref, parts_ref, front_ref, back_ref):
     row = lax.broadcasted_iota(jnp.int32, (8, LANES), 0) + (lax.axis_index("depth") >> 3) * 8
     limit = 8 * row + 8
-    slope = jnp.full((8, LANES), shear_ref[1], jnp.int32)
+    slope = slope_ref[...]
     zero = jnp.zeros((8, LANES), jnp.float32)
     reach = jnp.zeros((8, LANES), jnp.int32)
     total, front_total, front_light, back_light = zero, zero, zero, zero
     for d in range(DEPTH):
-        codes = parts_ref[d].astype(jnp.int32)
-        depth = depth_from_code(codes[:8], BRICK_RANGE)
-        light = from_code(codes[8:]) * depth * jnp.exp2(-total)
+        level, mean = unpair(parts_ref[d])
+        depth = depth_from_level(level, BRICK_RANGE)
+        light = mean * depth * jnp.exp2(-total)
         in_front = reach < limit
         front_total = jnp.where(in_front, front_total + depth, front_total)
         front_light = jnp.where(in_front, front_light + light, front_light)
@@ -219,23 +223,24 @@
     light = front_ref[8:16, :] + jnp.exp2(-front_ref[0:8, :]) * back_ref[8:16, :]
     opacity = 1.0 - jnp.exp2(-depth)
     mean = light / jnp.maximum(opacity, 2.0 ** IMAGE_RANGE[0])
-    codes = jnp.concatenate([depth_to_code(depth, IMAGE_RANGE), to_code(mean * TOP)], axis=0)
-    codes = codes.astype(jnp.int16)
+    codes = pair(depth_to_code(depth, IMAGE_RANGE), to_code(mean * TOP))
     for p in range(DEPTH):
         out_ref[p] = codes
 
 
 def image_kernel(palette_ref, whole_ref, image_hbm, image, sems):
-    base = [palette_ref[0, k] for k in range(3)]
-    slope = [palette_ref[1, k] for k in range(3)]
+    base, slope = [
+        [jnp.broadcast_to(palette_ref[i : i + 1, k : k + 1], (8, LANES)) for k in range(3)]
+        for i in range(2)
+    ]
     copies = []
     for g in range(ROWS // 8):
         rows = slice(g * 8, (g + 1) * 8)
         for j in range(BLOCKS):
             columns = slice(j * LANES, (j + 1) * LANES)
-            codes = whole_ref[g * BLOCKS + j].astype(jnp.int32)
-            opacity = 1.0 - jnp.exp2(-depth_from_code(codes[:8], IMAGE_RANGE))
-            light = from_code(codes[8:]) * (1.0 / TOP) * opacity
+            level, mean = unpair(whole_ref[g * BLOCKS + j])
+            opacity = 1.0 - jnp.exp2(-depth_from_level(level, IMAGE_RANGE))
+            light = mean * (1.0 / TOP) * opacity
             for k in range(3):
                 image[k, rows, columns] = base[k] * opacity + slope[k] * light
             image[3, rows, columns] = opacity
@@ -259,16 +264,17 @@
 
 def per_device(volume, empty_slices, shear, extinction, palette):
     f32 = jnp.float32
-    parts_shape = jax.ShapeDtypeStruct((DEPTH, 16, LANES), jnp.int16)
+    parts_shape = jax.ShapeDtypeStruct((DEPTH, 8, LANES), jnp.int32)
     piece_shape = jax.ShapeDtypeStruct((16, LANES), f32)
     down = [(i, i + 1) for i in range(TILES - 1)]
     first, last = lax.optimization_barrier((volume[:, :16, :], volume[:, ROWS - 16 :, :]))
     above = lax.ppermute(last[:, 14:, :].reshape(2 * SLAB, WIDTH), "tile", down)
-    turned, top = call(
+    turned, top, slope = call(
         bulk_kernel,
         (
             jax.ShapeDtypeStruct((2, BLOCKS, 2 * ROWS, LANES), f32),
             jax.ShapeDtypeStruct((SLAB, BLOCKS, 8, LANES), f32),
+            jax.ShapeDtypeStruct((8, LANES), jnp.int32),
         ),
         [SMEM, SMEM, SMEM, VMEM, VMEM],
         [pltpu.VMEM((SLAB, BLOCKS, HALO + ROWS, LANES), f32)],
@@ -283,7 +289,7 @@
         ],
     )(shear, extinction, empty_slices, top, above, turned)
     parts = lax.all_to_all(parts, "depth", 0, 0, tiled=True)
-    front, back = call(compose_kernel, (piece_shape, piece_shape), [SMEM, VMEM])(shear, parts)
+    front, back = call(compose_kernel, (piece_shape, piece_shape), [VMEM, VMEM])(slope, parts)
     back = lax.ppermute(back, "tile", down)
     copies = call(spread_kernel, parts_shape, [VMEM, VMEM])(front, back)
     whole = lax.all_to_all(copies, "depth", 0, 0, tiled=True)
@@ -291,7 +297,7 @@
     return call(
         image_kernel,
         image_shape,
-        [SMEM, VMEM],
+        [VMEM, VMEM],
         [
             pltpu.VMEM((4, ROWS, WIDTH), f32),
             pltpu.SemaphoreType.DMA((ROWS // 8,)),

time: 62 us -> 60.9 us (0.982)
  Pallas kernels: 6.94 us -> 5.87 us
    pallas_call x2, Pallas kernels: 2.4 us -> 1.37 us  [the longest x1 1.14 us: per_device(): call(image_kernel, image_shape, [VMEM, VMEM], [pltpu.VMEM((4, ROWS, WIDTH...]
where the time goes in v6:
time: 60.9 us; the launch traced here: 60.3 us
  blocking collectives  42.6 us (70%)
  starting transfers between devices  8.82 us (14%)
  Pallas kernels  5.87 us (10%)
  local copies, waits for them, and re-layouts  1.54 us (3%)
  waiting for transfers between devices  0.78 us (1%)
  between operations  0.74 us (1%)
    all_to_all x1, blocking collectives, per_device(): parts = lax.all_to_all(parts, 'depth', 0, 0, tiled=True)  24 us
    all_to_all x1, blocking collectives, per_device(): whole = lax.all_to_all(copies, 'depth', 0, 0, tiled=True)  18.5 us
    ppermute x1, starting transfers between devices, per_device(): above = lax.ppermute(last[:, 14:, :].reshape(2 * SLAB, WIDTH), 'tile', down)  4.83 us
    ppermute x1, starting transfers between devices, per_device(): back = lax.ppermute(back, 'tile', down)  4 us
    pallas_call x1, Pallas kernels, per_device(): call(bulk_kernel, (jax.ShapeDtypeStruct((2, BLOCKS, 2 * ROWS, LANES), f32...  3.19 us
    slice x1, local copies, waits for them, and re-layouts, per_device(): volume[:, ROWS - 16:, :]  1.43 us
    pallas_call x1, Pallas kernels, per_device(): call(edge_kernel, parts_shape, [SMEM, SMEM, SMEM, VMEM, VMEM, VMEM], [plt...  1.28 us
  transfers between devices with their start and end apart: 2, of which 1 were waited for; matrix products, arithmetic and copies ran while one was open for 0% of the time, Pallas kernels for 5%

profile of v6, /device:TPU:1, one launch (start us, length us, event | category | flops | bytes accessed | tf_op | source)
XLA Modules:
  0.0 60.3 jit_solution(3518201077996216220)
XLA Ops:
  0.0 0.0 copy-start
  0.0 0.0 copy-start.1
  0.0 0.0 copy-start.2
  0.0 1.4 %fusion = (bf16[16,16,1024]{2,1,0:T(8,128)(2,1)S(1)}, bf16[16,16,1024]{2,1,0:T(8,128)(2,1)S(1)}) fusion(bf16[16,64,1024]{2,1,0:T(8,128)(2,1)} %volume_ref.1), kind=kLoop, calls=%fused_computation | loop fusion | bytes 2097152 | tf_op jit(solution)/shard_map/slice | solution.py:270
  1.4 0.1 slice.11
  1.6 4.8 %collective-permute-start = (bf16[32,1024]{1,0:T(8,128)(2,1)S(1)}, bf16[32,1024]{1,0:T(8,128)(2,1)S(1)}, u32[]{:S(2)}, u32[]{:S(2)}) collective-permute-start(bf16[32,1024]{1,0:T(8,128)(2,1)S(1)} %reshape.3), channel_id=1, source_target_pairs={{0,1},{1,2},{2,3},{3,4},{4,5},{5,6},{6,7},{8,9},{9,10},{10,11},{11... | collective-permute-start | bytes 196616 | tf_op jit(solution)/shard_map/ppermute | solution.py:271
  7.0 0.0 copy-done
  7.1 0.0 copy-done.1
  7.1 0.0 copy-done.2
  7.1 3.2 %shard_map.55 = (f32[2,8,128,128]{3,2,1,0:T(8,128)S(1)}, f32[16,8,8,128]{3,2,1,0:T(8,128)S(1)}, s32[8,128]{1,0:T(8,128)S(1)}) custom-call(s32[2]{0:T(128)S(1)} %copy-done.1, f32[1]{0:T(128)S(6)} %copy.6.ext_ref, s32[1,8]{1,0:T(1,128)S(1)} %copy-done.2, bf16[16,16,1024]{2,1,0:T(8,128)(2,1)S(1)} %get-tuple-element.12.first_ref, bf16[16,64,1024]{2,1,0:T(8,128)(2,1)S(1)} %copy-done), custom_call_target="tpu_custom_call" | custom-call | tf_op jit(solution)/shard_map/pallas_call | solution.py:272
  10.3 0.0 copy-start.3
  10.3 0.0 collective-permute-done.above_ref
  10.3 1.3 %shard_map.56 = s32[64,8,128]{2,1,0:T(8,128)S(1)} custom-call(s32[2]{0:T(128)S(1)} %copy-done.1, f32[1]{0:T(128)S(6)} %copy.6.ext_ref, s32[1,8]{1,0:T(1,128)S(1)} %copy-done.2, f32[16,8,8,128]{3,2,1,0:T(8,128)S(1)} %get-tuple-element.14.top_ref, bf16[32,1024]{1,0:T(8,128)(2,1)S(1)} %collective-permute-done.above_ref, ...), custom_call_target="tpu_custom_call" | custom-call | tf_op jit(solution)/shard_map/pallas_call | solution.py:282
  11.6 24.0 %all_to_all.10.parts_ref = s32[64,8,128]{2,1,0:T(8,128)S(1)} all-to-all(s32[64,8,128]{2,1,0:T(8,128)S(1)} %shard_map.56), channel_id=1, replica_groups=mesh['depth'=64,'tile'=8] {'depth'}, dimensions={0} | all-to-all | bytes 524288 | tf_op jit(solution)/shard_map/all_to_all | solution.py:291
  35.6 0.2 shard_map.57
  35.8 4.0 %collective-permute-start.1 = (f32[16,128]{1,0:T(8,128)S(1)}, f32[16,128]{1,0:T(8,128)S(1)}, u32[]{:S(2)}, u32[]{:S(2)}) collective-permute-start(f32[16,128]{1,0:T(8,128)S(1)} %get-tuple-element.18), channel_id=1, source_target_pairs={{0,1},{1,2},{2,3},{3,4},{4,5},{5,6},{6,7},{8,9},{9,10},{10,11},{11... | collective-permute-start | bytes 24584 | tf_op jit(solution)/shard_map/ppermute | solution.py:293
  39.8 0.8 %collective-permute-done.1.back_ref = f32[16,128]{1,0:T(8,128)S(1)} collective-permute-done((f32[16,128]{1,0:T(8,128)S(1)}, f32[16,128]{1,0:T(8,128)S(1)}, u32[]{:S(2)}, u32[]{:S(2)}) %collective-permute-start.1) | collective-permute-done | bytes 8224 | tf_op jit(solution)/shard_map/ppermute | solution.py:293
  40.7 18.5 %all_to_all.11.whole_ref = s32[64,8,128]{2,1,0:T(8,128)S(1)} all-to-all(s32[64,8,128]{2,1,0:T(8,128)S(1)} %shard_map.58), channel_id=1, replica_groups=mesh['depth'=64,'tile'=8] {'depth'}, dimensions={0} | all-to-all | bytes 524288 | tf_op jit(solution)/shard_map/all_to_all | solution.py:295
  59.2 0.0 copy-done.3
  59.2 1.1 %shard_map.59 = f32[4,64,1024]{2,1,0:T(8,128)} custom-call(f32[2,3]{1,0:T(2,128)S(1)} %copy-done.3, s32[64,8,128]{2,1,0:T(8,128)S(1)} %all_to_all.11.whole_ref), custom_call_target="tpu_custom_call" | custom-call | tf_op jit(solution)/shard_map/pallas_call | solution.py:297
  (2 shorter events, 0.1 us)
Async XLA Ops:
  0.0 7.0 %copy-start = (bf16[16,64,1024]{2,1,0:T(8,128)(2,1)S(1)}, bf16[16,64,1024]{2,1,0:T(8,128)(2,1)}, u32[]{:S(2)}) copy-start(bf16[16,64,1024]{2,1,0:T(8,128)(2,1)} %volume_ref.1) | copy-start | bytes 6291460
  0.0 7.1 %copy-start.1 = (s32[2]{0:T(128)S(1)}, s32[2]{0:T(128)}, u32[]{:S(2)}) copy-start(s32[2]{0:T(128)} %shear_ref.3) | copy-start | bytes 28
  0.0 7.1 %copy-start.2 = (s32[1,8]{1,0:T(1,128)S(1)}, s32[1,8]{1,0:T(1,128)}, u32[]{:S(2)}) copy-start(s32[1,8]{1,0:T(1,128)} %empty_ref.3) | copy-start | bytes 100
  1.6 8.7 %collective-permute-start = (bf16[32,1024]{1,0:T(8,128)(2,1)S(1)}, bf16[32,1024]{1,0:T(8,128)(2,1)S(1)}, u32[]{:S(2)}, u32[]{:S(2)}) collective-permute-start(bf16[32,1024]{1,0:T(8,128)(2,1)S(1)} %reshape.3), channel_id=1, source_target_pairs={{0,1},{1,2},{2,3},{3,4},{4,5},{5,6},{6,7},{8,9},{9,10},{10,11},{11... | collective-permute-start | bytes 196616 | tf_op jit(solution)/shard_map/ppermute | solution.py:271
  10.3 48.9 %copy-start.3 = (f32[2,3]{1,0:T(2,128)S(1)}, f32[2,3]{1,0:T(2,128)}, u32[]{:S(2)}) copy-start(f32[2,3]{1,0:T(2,128)} %palette_ref.1) | copy-start | bytes 76
  35.8 4.8 %collective-permute-start.1 = (f32[16,128]{1,0:T(8,128)S(1)}, f32[16,128]{1,0:T(8,128)S(1)}, u32[]{:S(2)}, u32[]{:S(2)}) collective-permute-start(f32[16,128]{1,0:T(8,128)S(1)} %get-tuple-element.18), channel_id=1, source_target_pairs={{0,1},{1,2},{2,3},{3,4},{4,5},{5,6},{6,7},{8,9},{9,10},{10,11},{11... | collective-permute-start | bytes 24584 | tf_op jit(solution)/shard_map/ppermute | solution.py:293
